TPU v7x, 256 devices: a whole 4x4x8 slice. The times are simulated.
256 devices in a mesh: row: 16 (over x, y), col: 16 (over z, core).
Axes of the slice: x: 4, y: 4, z: 8, core: 2. Of those that a mesh axis runs over, the one named last changes fastest.
Arguments:
- features: bfloat16 [32768, 512], P('col', 'row'), may hold values from -6 to 6
- weight: bfloat16 [512, 512], replicated, may hold values from -0.25 to 0.25
- block_cols: int32 [256, 16, 8], P('row', 'col'), may hold values from 0 to 15
- block_count: int32 [256, 16], P('row', 'col'), may hold values from 1 to 8
- edge_src: int32 [256, 16, 8, 512], P('row', 'col'), may hold values from 0 to 127
- edge_dst: int32 [256, 16, 8, 512], P('row', 'col'), may hold values from 0 to 127
- edge_weight: bfloat16 [256, 16, 8, 512], P('row', 'col'), may hold values from 0.099609375 to 0.5
- cotangent: bfloat16 [32768, 512], P('row', 'col'), may hold values from -6 to 6
Outputs:
- activated: bfloat16 [32768, 512], P('row', 'col')
- feature_grad: bfloat16 [32768, 512], P('col', 'row')
- weight_grad: float32 [512, 512], replicated
Inputs may be any that keep to these rules, and one draw needn't show every extreme that they name: `block_cols`: column blocks are numbered within their column group; the same block may appear in several slots.
All inputs are finite; a program needn't handle non-finite values.
Results may differ from a plain program's by a relative error of at most 0.0069.
Values may be sent and summed in bfloat16 or wider, within the bound.
A program may use at most 192 MiB of HBM per device.

v0:
```python
import jax
import jax.numpy as jnp
from jax import lax
from jax.sharding import PartitionSpec as P


def make_tiles(edge_src, edge_dst, edge_weight, counts):
    kmax = edge_src.shape[1]
    slots = jnp.arange(kmax, dtype=jnp.int32)
    lanes = jnp.arange(128, dtype=jnp.int32)

    def one_block(args):
        src, dst, wts, count = args
        live = (slots < count).astype(jnp.bfloat16)
        scaled = wts * live[:, None]
        left = (dst[:, :, None] == lanes).astype(jnp.bfloat16) * scaled[:, :, None]
        right = (src[:, :, None] == lanes).astype(jnp.bfloat16)
        tiles = jnp.einsum("kea,keb->kab", left, right, preferred_element_type=jnp.float32)
        return tiles.astype(jnp.bfloat16)

    return lax.map(one_block, (edge_src, edge_dst, edge_weight, counts))


def shards(features, weight, block_cols, block_count, edge_src, edge_dst, edge_weight, cotangent):
    width = weight.shape[1]
    columns = block_cols[:, 0, :]
    counts = block_count[:, 0]
    rows_b = columns.shape[0]
    kmax = columns.shape[1]
    col_rows = features.shape[0]
    cbl = col_rows // 128
    share_rows = features.shape[1]
    tiles = make_tiles(edge_src[:, 0], edge_dst[:, 0], edge_weight[:, 0], counts)
    projected = jnp.dot(
        lax.all_gather(features, "row", axis=1, tiled=True),
        weight,
        preferred_element_type=jnp.float32,
    )
    proj_blocks = projected.astype(jnp.bfloat16).reshape(cbl, 128, width)

    def forward_block(args):
        tile_set, index = args
        picked = proj_blocks[index]
        return jnp.einsum("kab,kbf->af", tile_set, picked, preferred_element_type=jnp.float32)

    partial_rows = lax.map(forward_block, (tiles, columns)).reshape(rows_b * 128, width)
    hidden = lax.psum_scatter(partial_rows, "col", scatter_dimension=1, tiled=True)
    sig = jax.nn.sigmoid(hidden)
    activated = (hidden * sig).astype(jnp.bfloat16)
    slope = (cotangent.astype(jnp.float32) * sig * (1.0 + hidden * (1.0 - sig))).astype(
        jnp.bfloat16
    )
    placing = (
        jnp.arange(cbl, dtype=jnp.int32)[:, None] == columns.reshape(1, rows_b * kmax)
    ).astype(jnp.float32)
    piece = lax.all_gather(slope, "col", axis=1, tiled=True)
    span = piece.shape[1]
    blocks = piece.reshape(rows_b, 128, span)
    parts = jnp.einsum("gkab,gaf->gkbf", tiles, blocks, preferred_element_type=jnp.float32)
    flat = parts.reshape(rows_b * kmax, 128 * span)
    total = jnp.dot(
        placing, flat, precision=lax.Precision.HIGHEST, preferred_element_type=jnp.float32
    )
    term = total.reshape(col_rows, span)
    back = lax.psum(term, "row").astype(jnp.bfloat16)
    offset = lax.axis_index("row") * share_rows
    weight_rows = lax.dynamic_slice_in_dim(weight, offset, share_rows, 0)
    feature_grad = lax.dot_general(
        back, weight_rows, (((1,), (1,)), ((), ())), preferred_element_type=jnp.float32
    ).astype(jnp.bfloat16)
    grad_term = lax.dot_general(
        features, back, (((0,), (0,)), ((), ())), preferred_element_type=jnp.float32
    )
    summed = lax.psum(grad_term, "col")
    weight_grad = lax.all_gather(summed, "row", axis=0, tiled=True)
    return (activated, feature_grad, weight_grad)


def solution(mesh):
    return jax.shard_map(
        shards,
        mesh=mesh,
        in_specs=(
            P("col", "row"),
            P(),
            P("row", "col", None),
            P("row", "col"),
            P("row", "col", None, None),
            P("row", "col", None, None),
            P("row", "col", None, None),
            P("row", "col"),
        ),
        out_specs=(P("row", "col"), P("col", "row"), P()),
        check_vma=False,
    )
```

profile of v0, /device:TPU:1, one launch (start us, length us, event | category | flops | bytes accessed | tf_op | source)
XLA Modules:
  0.0 595.6 jit_solution(3819947424413958949)
XLA Ops:
  8.0 75.9 %while.23 = (s32[]{:T(128)}, bf16[16,8,128,128]{3,2,1,0:T(8,128)(2,1)}, s32[16,8,512]{2,1,0:T(8,128)}, bf16[16,8,512]{2,1,0:T(8,128)(2,1)}, s32[16]{0:T(128)}, /*index=5*/s32[16,8,512]{2,1,0:T(8,128)}, s32[]{:T(128)}) while((s32[]{:T(128)}, bf16[16,8,128,128]{3,2,1,0:T(8,128)(2,1)}, s32[16,8,512]{2,1,0:T(8,128)}, ...), condition=%wide.region_1.2_spmd.clone.clone, body=%wide.region_0.1_spmd.clone.clone.sunk | while | flops 135925776 | bytes 385169 | solution.py:21
  83.9 4.2 convolution_convert_fusion
  88.2 67.3 %while.22 = (s32[]{:T(128)}, f32[16,128,512]{2,1,0:T(8,128)}, bf16[16,8,128,128]{3,2,1,0:T(8,128)(2,1)}, s32[16,8]{1,0:T(8,128)S(1)}, bf16[16,128,512]{2,1,0:T(8,128)(2,1)}, /*index=5*/s32[]{:T(128)}) while((s32[]{:T(128)}, f32[16,128,512]{2,1,0:T(8,128)}, bf16[16,8,128,128]{3,2,1,0:T(8,128)(2,1)}, s32[16,8]{1,0:T(8,128)S(1)}, ...), condition=%wide.region_3.4_spmd, body=%wide.region_2.3_spmd.sunk | while | flops 134218784 | bytes 3675345 | solution.py:46
  88.2 2.2 gather_fusion
  90.4 2.0 fusion.45
  92.4 2.2 gather_fusion
  94.6 2.0 fusion.45
  96.6 2.2 gather_fusion
  98.8 2.0 fusion.45
  100.8 2.2 gather_fusion
  103.0 2.0 fusion.45
  105.0 2.2 gather_fusion
  107.2 2.0 fusion.45
  109.2 2.2 gather_fusion
  111.4 2.0 fusion.45
  113.4 2.2 gather_fusion
  115.6 2.0 fusion.45
  117.6 2.2 gather_fusion
  119.8 2.0 fusion.45
  121.8 2.2 gather_fusion
  124.1 2.0 fusion.45
  126.1 2.2 gather_fusion
  128.3 2.0 fusion.45
  130.3 2.2 gather_fusion
  132.5 2.0 fusion.45
  134.5 2.2 gather_fusion
  136.7 2.0 fusion.45
  138.7 2.2 gather_fusion
  140.9 2.0 fusion.45
  142.9 2.2 gather_fusion
  145.1 2.0 fusion.45
  147.1 2.2 gather_fusion
  149.3 2.0 fusion.45
  151.3 2.2 gather_fusion
  153.5 2.0 fusion.45
  155.5 5.4 copy.26
  161.0 63.5 %reduce-scatter.2.cloned.1.call-done = f32[2048,32]{0,1:T(8,128)} async-done(((f32[2048,512]{0,1:T(8,128)}), f32[2048,32]{0,1:T(8,128)}) %reduce-scatter.2.cloned.1.call-update) | async-done | bytes 262160 | tf_op jit(solution)/shard_map/reduce_scatter | solution.py:47
  224.4 1.8 multiply_convert_fusion
  226.6 42.1 %all-gather.6.cloned.1.call-done = bf16[2048,512]{0,1:T(8,128)(2,1)} async-done(((bf16[2048,32]{0,1:T(8,128)(2,1)}), bf16[2048,512]{0,1:T(8,128)(2,1)}) %all-gather.6.cloned.1.call-update) | async-done | bytes 2097168 | tf_op jit(solution)/shard_map/all_gather | solution.py:56
  268.7 2.9 copy.21
  271.6 15.5 %convolution_bitcast_fusion.1 = f32[16,8,128,512]{3,2,1,0:T(8,128)} fusion(bf16[16,8,128,128]{3,2,1,0:T(8,128)(2,1)} %get-tuple-element.270, bf16[16,128,512,1]{2,1,3,0:T(8,128)(2,1)S(1)} %bitcast.75), kind=kOutput, calls=%fused_computation.29 | convolution fusion | flops 2147483648 | bytes 39845888 | tf_op jit(solution)/shard_map/gkab,gaf->gkbf/dot_general | solution.py:59
  287.1 31.7 %copy.27 = f32[16,8,128,512]{3,1,2,0:T(8,128)} copy(f32[16,8,128,512]{3,2,1,0:T(8,128)} %convolution_bitcast_fusion.1) | data formatting | bytes 67108864
  318.8 16.7 %fusion.24 = f32[16,65536]{1,0:T(8,128)} fusion(f32[128,65536]{1,0:T(8,128)} %bitcast.74, s32[128]{0:T(128)S(1)} %eq.46), kind=kOutput, calls=%fused_computation.40 | convolution fusion | flops 1610614784 | bytes 37749248 | tf_op jit(solution)/shard_map/dot_general | solution.py:61
  335.6 3.9 reshape.82
  339.5 100.8 %all-reduce.4 = bf16[2048,512]{1,0:T(8,128)(2,1)S(1)} all-reduce(f32[2048,512]{1,0:T(8,128)} %reshape.82), channel_id=1, replica_groups=mesh['row'=16,'col'=16] {'row'}, use_global_device_ids=true, to_apply=%region_5.6 | all-reduce | flops 1048576 | bytes 6291456 | tf_op jit(solution)/shard_map/psum | solution.py:65
  441.5 98.2 %all-reduce.3.cloned.1.call-done = f32[32,512]{1,0:T(8,128)} async-done(((f32[32,512]{1,0:T(8,128)}), f32[32,512]{1,0:T(8,128)}) %all-reduce.3.cloned.1.call-update) | async-done | bytes 65552 | tf_op jit(solution)/shard_map/psum | solution.py:74
  541.2 45.6 %all-gather.8.cloned.1.call-done = f32[512,512]{1,0:T(8,128)} async-done(((f32[32,512]{1,0:T(8,128)}), f32[512,512]{1,0:T(8,128)}) %all-gather.8.cloned.1.call-update) | async-done | bytes 1048592 | tf_op jit(solution)/shard_map/all_gather | solution.py:75
  586.8 2.3 copy.46
  (138 shorter events, 79.8 us)
Async XLA Ops:
  7.2 76.8 %copy-start = (bf16[512,512]{1,0:T(8,128)(2,1)S(1)}, bf16[512,512]{1,0:T(8,128)(2,1)}, u32[]{:S(2)}) copy-start(bf16[512,512]{1,0:T(8,128)(2,1)} %param.13) | copy-start | bytes 1572868
  7.2 76.7 %all-gather.4.cloned.1.call-start = ((), (), s32[]{:S(2)}) async-start(), calls=%async_computation.1 | async-start | bytes 2228224 | tf_op jit(solution)/shard_map/all_gather | solution.py:35
  7.9 216.5 %reduce-scatter.2.cloned.1.call-start = ((), (), s32[]{:S(2)}) async-start(), calls=%async_computation.2 | async-start | bytes 4456448 | tf_op jit(solution)/shard_map/reduce_scatter | solution.py:47
  8.0 75.9 %copy-start.3 = (s32[16,1,8]{0,2,1:T(8,128)S(1)}, s32[16,1,8]{0,2,1:T(8,128)}, u32[]{:S(2)}) copy-start(s32[16,1,8]{0,2,1:T(8,128)} %param.14) | copy-start | bytes 1540
  160.9 63.5 %copy-start.2 = (bf16[2048,32]{0,1:T(8,128)(2,1)S(1)}, bf16[2048,32]{0,1:T(8,128)(2,1)}, u32[]{:S(2)}) copy-start(bf16[2048,32]{0,1:T(8,128)(2,1)} %param.19) | copy-start | bytes 393220
  160.9 107.8 %all-gather.6.cloned.1.call-start = ((), (), s32[]{:S(2)}) async-start(), calls=%async_computation.3 | async-start | bytes 2228224 | tf_op jit(solution)/shard_map/all_gather | solution.py:56
  226.2 313.5 %all-reduce.3.cloned.1.call-start = ((), (), s32[]{:S(2)}) async-start(), calls=%async_computation.4 | async-start | bytes 131072 | tf_op jit(solution)/shard_map/psum | solution.py:74
  339.5 100.8 %copy-start.1 = (bf16[2048,32]{0,1:T(8,128)(2,1)S(1)}, bf16[2048,32]{0,1:T(8,128)(2,1)}, u32[]{:S(2)}) copy-start(bf16[2048,32]{0,1:T(8,128)(2,1)} %param.12) | copy-start | bytes 393220
  441.5 145.3 %all-gather.8.cloned.1.call-start = ((), (), s32[]{:S(2)}) async-start(), calls=%async_computation.5 | async-start | bytes 1114112 | tf_op jit(solution)/shard_map/all_gather | solution.py:75
Sparse Core Ops, SparseCore 0:
  10.4 53.0 all-gather.3
  161.0 63.3 reduce-scatter.1
  226.8 41.8 all-gather.5
  441.6 98.1 all-reduce.2
  542.3 44.4 all-gather.7
where the time goes:
time: 600 us; the launch traced here: 596 us
  waiting for transfers between devices  250 us (42%)
  local copies, waits for them, and re-layouts  113 us (19%)
  blocking collectives  101 us (17%)
  matrix products  91.9 us (15%)
  other arithmetic  24.8 us (4%)
  between operations  13.8 us (2%)
    psum x1, blocking collectives, shards(): back = lax.psum(term, 'row').astype(jnp.bfloat16)  101 us
    psum x1, waiting for transfers between devices, shards(): summed = lax.psum(grad_term, 'col')  98.2 us
    reduce_scatter x1, waiting for transfers between devices, shards(): lax.psum_scatter(partial_rows, 'col', scatter_dimension=1, tiled=True)  63.5 us
    all_gather x1, waiting for transfers between devices, shards(): weight_grad = lax.all_gather(summed, 'row', axis=0, tiled=True)  45.6 us
    all_gather x1, waiting for transfers between devices, shards(): piece = lax.all_gather(slope, 'col', axis=1, tiled=True)  42.1 us
    gather x16, local copies, waits for them, and re-layouts, forward_block(): picked = proj_blocks[index]  35.3 us
    unnamed x11, local copies, waits for them, and re-layouts  34.1 us
    dot_general x16, matrix products, forward_block(): jnp.einsum('kab,kbf->af', tile_set, picked, preferred_element_type=jnp.fl...  31.6 us
  transfers between devices with their start and end apart: 5, of which 4 were waited for; matrix products, arithmetic and copies ran while one was open for 13% of the time, Pallas kernels for 0%

commit v1 on v0

v1 whole, which is shorter than its diff:
```python
import jax
import jax.numpy as jnp
from jax import lax
from jax.experimental import pallas as pl
from jax.experimental.pallas import tpu as pltpu
from jax.sharding import PartitionSpec as P

MESH = pl.DeviceIdType.MESH
BF = jnp.bfloat16
F32 = jnp.float32
NT = (((1,), (1,)), ((), ()))
TN = (((0,), (0,)), ((), ()))
NS = 2
SUB = 512 // NS


def build_kernel(cols_ref, counts_ref, src_ref, dst_ref, w_ref, out_ref):
    g = pl.program_id(0)
    out_ref[...] = jnp.zeros_like(out_ref)
    spots = lax.broadcasted_iota(jnp.int32, (128, 512), 0).astype(F32).astype(BF)
    src = src_ref[0].astype(F32)
    dst = dst_ref[0].astype(F32)
    wts = w_ref[0].astype(F32)
    one = jnp.ones((128, 512), BF)
    zero = jnp.zeros((128, 512), BF)

    def spread(row):
        piece = jnp.broadcast_to(row, (16, 512)).astype(BF)
        return jnp.concatenate([piece] * 8, axis=0)

    for k in range(8):

        @pl.when(k < counts_ref[g])
        def _():
            left = jnp.where(spots == spread(dst[k : k + 1]), spread(wts[k : k + 1]), zero)
            right = jnp.where(spots == spread(src[k : k + 1]), one, zero)
            tile = lax.dot_general(left, right, NT, preferred_element_type=F32).astype(BF)
            where = pl.ds(pl.multiple_of(cols_ref[g, k] * 128, 128), 128)
            out_ref[:, where] = out_ref[:, where] + tile


def build(cols, counts, src, dst, wts):
    return pl.pallas_call(
        build_kernel,
        out_shape=jax.ShapeDtypeStruct((2048, 2048), BF),
        grid_spec=pltpu.PrefetchScalarGridSpec(
            num_scalar_prefetch=2,
            grid=(16,),
            in_specs=[pl.BlockSpec((1, 8, 512), lambda g, *_: (g, 0, 0))] * 3,
            out_specs=pl.BlockSpec((128, 2048), lambda g, *_: (g, 0)),
        ),
        name="build",
    )(cols, counts, src, dst, wts)


def layer_kernel(
    xt_ref, cot_ref, w_ref, a_hbm,
    act_ref, fg_ref, wg_ref,
    a, xg, cotb, pown, psend, precv, zr, zs, axb, actb, slb, tg, acc,
    xs1, xr1h, xr1f, s1, xs2, xr2h, xr2f,
    wp, wr, wz,
    a_sem, loc_sem,
    cot_ss, cot_rs, ag_ss, ag_rs, core_ss, core_rs, rz_ss, rz_rs,
    act_ss, act_rs, gz_ss, gz_rs, gc_ss, gc_rs, rx_ss, rx_rs,
    w1_ss, w1_rs, w2_ss, w2_rs, w3_ss, w3_rs,
):
    r = lax.axis_index("row")
    c = lax.axis_index("col")
    x, y = r // 4, r % 4
    z, k = c // 2, c % 2

    def at_x(o):
        return ((x + o) % 4 * 4 + y, c)

    def at_y(o):
        return (x * 4 + (y + o) % 4, c)

    def at_z(o):
        return (r, (z + o) % 8 * 2 + k)

    twin = (r, z * 2 + 1 - k)

    def rc(src, dst, ss, rs, dev):
        return pltpu.make_async_remote_copy(
            src_ref=src, dst_ref=dst, send_sem=ss, recv_sem=rs, device_id=dev, device_id_type=MESH
        )

    sent = []

    def send(src, dst, ss, rs, dev):
        copy = rc(src, dst, ss, rs, dev)
        copy.start()
        sent.append(copy)

    def got(ref, ss, rs, dev):
        rc(ref, ref, ss, rs, dev).wait_recv()

    barrier = pltpu.get_barrier_semaphore()

    def greet(i, _):
        pl.semaphore_signal(barrier, inc=1, device_id=((r + i) % 16, c), device_id_type=MESH)
        pl.semaphore_signal(barrier, inc=1, device_id=(r, (c + i) % 16), device_id_type=MESH)
        return 0

    lax.fori_loop(1, 16, greet, 0)
    a_copy = pltpu.make_async_copy(a_hbm, a, a_sem)
    a_copy.start()
    for h in (0, 1):
        xg[h, x, y] = xt_ref[:, h * 1024 : (h + 1) * 1024]
    pl.semaphore_wait(barrier, 30)

    def xg_at(h, o1, o2):
        if h == 0:
            return xg.at[0, (x + o2) % 4, (y + o1) % 4]
        return xg.at[1, (x + o1) % 4, (y + o2) % 4]

    def axis(h, ring):
        return (at_y, at_x)[(h + ring) % 2]

    def ag_send(h, ring, lane, j, piece):
        dev = axis(h, ring)(1 if j % 2 == 0 else -1)
        if j == 2:
            piece = piece.at[0:16]
        if j == 3:
            piece = piece.at[16:32]
        send(piece, piece, ag_ss.at[h, lane, j], ag_rs.at[h, lane, j], dev)

    def ag_got(h, ring, lane, j, piece):
        dev = axis(h, ring)(-1 if j % 2 == 0 else 1)
        if j == 2:
            piece = piece.at[0:16]
        if j == 3:
            piece = piece.at[16:32]
        got(piece, ag_ss.at[h, lane, j], ag_rs.at[h, lane, j], dev)

    def ag_ring2_own(h, o1):
        for j in (0, 1):
            ag_send(h, 1, 1 + o1, j, xg_at(h, o1, 0))

    def ag_ring2_pass(h, o1):
        for j, o in ((0, 3), (1, 1)):
            ag_got(h, 1, 1 + o1, j, xg_at(h, o1, o))
            ag_send(h, 1, 1 + o1, 2 + j, xg_at(h, o1, o))

    for h in (0, 1):
        for j in (0, 1):
            ag_send(h, 0, 0, j, xg_at(h, 0, 0))
    for h in (0, 1):
        ag_ring2_own(h, 0)

    def cot_copy(i, peer, mine):
        return rc(
            cot_ref.at[:, pl.ds(pl.multiple_of(peer * 128, 128), 128)],
            cotb.at[pl.ds(pl.multiple_of(mine * 32, 32), 32), :],
            cot_ss.at[i], cot_rs.at[i], (r, peer),
        )

    def cot_send(i, _):
        cot_copy(i, (c + i) % 16, c).start()
        return 0

    lax.fori_loop(1, 16, cot_send, 0)
    cotb[pl.ds(pl.multiple_of(c * 32, 32), 32), :] = cot_ref[:, pl.ds(pl.multiple_of(c * 128, 128), 128)]

    for j, o in ((0, 3), (1, 1)):
        for h in (0, 1):
            ag_got(h, 0, 0, j, xg_at(h, o, 0))
            ag_send(h, 0, 0, 2 + j, xg_at(h, o, 0))
            ag_ring2_own(h, o)
    for h in (0, 1):
        ag_ring2_pass(h, 0)
    for h in (0, 1):
        for j in (2, 3):
            ag_got(h, 0, 0, j, xg_at(h, 2, 0))
        ag_ring2_own(h, 2)
    for o1 in (3, 1, 2):
        for h in (0, 1):
            ag_ring2_pass(h, o1)
    for o1 in (0, 3, 1, 2):
        for h in (0, 1):
            for j in (2, 3):
                ag_got(h, 1, 1 + o1, j, xg_at(h, o1, 2))
    a_copy.wait()

    def product(d):
        rows = pl.ds(pl.multiple_of((z + d) % 8 * 256, 256), 256)
        total = lax.dot_general(
            xg[0].reshape(512, 1024), a[rows, 0:1024], NT, preferred_element_type=F32
        ) + lax.dot_general(
            xg[1].reshape(512, 1024), a[rows, 1024:2048], NT, preferred_element_type=F32
        )
        low, high = total[:, 0:128], total[:, 128:256]
        first = k == 0
        pown[d] = jnp.where(first, low, high)
        psend[d] = jnp.where(first, high, low).astype(BF)
        send(psend.at[d], precv.at[d], core_ss.at[d], core_rs.at[d], twin)

    def twin_got(d):
        got(precv.at[d], core_ss.at[d], core_rs.at[d], twin)

    def z_rows(side, dist, j):
        return dist < 4 or (j < NS // 2) == (side == 0)

    def z_step(dist):
        offsets = (4,) if dist == 4 else (dist, 8 - dist)
        for d in offsets:
            twin_got(d)
        for j in range(NS):
            rows = pl.ds(j * SUB, SUB)
            for side in (0, 1):
                if not z_rows(side, dist, j):
                    continue
                d = dist if side == 0 else (8 - dist) % 8
                value = pown[d, rows] + precv[d, rows].astype(F32)
                if dist < 4 and z_rows(side, dist + 1, j):
                    got(zr.at[side, dist, rows], rz_ss.at[side, dist + 1, j], rz_rs.at[side, dist + 1, j], at_z(-1 if side == 0 else 1))
                    value = value + zr[side, dist, rows].astype(F32)
                zs[side, dist, rows] = value.astype(BF)
                send(
                    zs.at[side, dist, rows], zr.at[side, dist - 1, rows],
                    rz_ss.at[side, dist, j], rz_rs.at[side, dist, j], at_z(1 if side == 0 else -1),
                )

    product(4)
    product(3)
    product(5)
    z_step(4)
    product(2)
    product(6)
    z_step(3)
    product(1)
    product(7)
    z_step(2)
    product(0)
    z_step(1)
    twin_got(0)
    for j in range(NS):
        rows = pl.ds(j * SUB, SUB)
        value = pown[0, rows] + precv[0, rows].astype(F32)
        for side in (0, 1):
            got(zr.at[side, 0, rows], rz_ss.at[side, 1, j], rz_rs.at[side, 1, j], at_z(-1 if side == 0 else 1))
            value = value + zr[side, 0, rows].astype(F32)
        axb[rows] = value.astype(BF)

    def cot_wait(i, _):
        cot_copy(i, c, (c + 16 - i) % 16).wait_recv()
        return 0

    lax.fori_loop(1, 16, cot_wait, 0)
    hidden = lax.dot_general(w_ref[...], axb[...], TN, preferred_element_type=F32)
    sig = jax.nn.sigmoid(hidden)
    actb[...] = (hidden * sig).astype(BF)
    slb[...] = (cotb[...].astype(F32) * sig * (1.0 + hidden * (1.0 - sig))).astype(BF)
    tg[z, k] = jnp.dot(w_ref[...], slb[...], preferred_element_type=F32).astype(BF)

    def gz_send(side, dist, j):
        owner = (z - dist + 8) % 8 if side == 0 else (z + dist) % 8
        piece = tg.at[owner, k, pl.ds(j * SUB, SUB)]
        send(piece, piece, gz_ss.at[side, dist, j], gz_rs.at[side, dist, j], at_z(1 if side == 0 else -1))

    def gz_got(side, dist, j):
        owner = (z - dist + 8) % 8 if side == 0 else (z + dist) % 8
        piece = tg.at[owner, k, pl.ds(j * SUB, SUB)]
        got(piece, gz_ss.at[side, dist - 1, j], gz_rs.at[side, dist - 1, j], at_z(-1 if side == 0 else 1))

    def gc_send(d):
        piece = tg.at[(z + d) % 8, k]
        send(piece, piece, gc_ss.at[d], gc_rs.at[d], twin)

    def gc_got(d):
        piece = tg.at[(z + d) % 8, 1 - k]
        got(piece, gc_ss.at[d], gc_rs.at[d], twin)

    for j in range(NS):
        for side in (0, 1):
            gz_send(side, 0, j)
    gc_send(0)

    def act_copy(i, peer, mine):
        return rc(
            actb.at[pl.ds(pl.multiple_of(peer * 32, 32), 32), :],
            act_ref.at[:, pl.ds(pl.multiple_of(mine * 128, 128), 128)],
            act_ss.at[i], act_rs.at[i], (r, peer),
        )

    def act_send(i, _):
        act_copy(i, (c + i) % 16, c).start()
        return 0

    lax.fori_loop(1, 16, act_send, 0)
    act_ref[:, pl.ds(pl.multiple_of(c * 128, 128), 128)] = actb[pl.ds(pl.multiple_of(c * 32, 32), 32), :]

    wp[...] = lax.dot_general(axb[...], slb[...], NT, preferred_element_type=F32).astype(BF)

    def w_rows(i):
        return pl.ds(pl.multiple_of(i * 32, 32), 32)

    def w1_copy(i, peer, mine):
        return rc(wp.at[w_rows(peer)], wr.at[mine], w1_ss.at[i], w1_rs.at[i], (peer, c))

    def w1_send(i, _):
        w1_copy(i, (r + i) % 16, r).start()
        return 0

    lax.fori_loop(1, 16, w1_send, 0)
    wr[r] = wp[w_rows(r)]

    def gather_step(dist):
        for j in range(NS):
            for side in (0, 1):
                if not z_rows(side, dist, j):
                    continue
                gz_got(side, dist, j)
                if dist < 4 and z_rows(side, dist + 1, j):
                    gz_send(side, dist, j)
        for d in (4,) if dist == 4 else (dist, 8 - dist):
            gc_send(d)

    def back_part(d):
        block = (z + d) % 8
        left = jnp.concatenate([tg[block, 0], tg[block, 1]], axis=1)
        rows = pl.ds(pl.multiple_of(block * 256, 256), 256)
        return jnp.dot(left, a[rows, :], preferred_element_type=F32)

    gc_got(0)
    acc[...] = back_part(0)
    for dist in (1, 2, 3, 4):
        gather_step(dist)
        for d in (4,) if dist == 4 else (dist, 8 - dist):
            gc_got(d)
            acc[...] += back_part(d)

    def q_rows(h, o1, o2):
        if h == 0:
            block = (x + o1) % 4 * 4 + (y + o2) % 4
        else:
            block = (x + o2) % 4 * 4 + (y + o1) % 4
        return block * 32

    def q(h, o1, o2, half):
        start = q_rows(h, o1, o2)
        if half is None:
            return acc[pl.ds(pl.multiple_of(start, 32), 32), h * 1024 : (h + 1) * 1024]
        return acc[pl.ds(pl.multiple_of(start + 16 * half, 16), 16), h * 1024 : (h + 1) * 1024]

    def rx_axis(h, ring):
        return (at_x, at_y)[(h + ring) % 2]

    def rx(src, dst, h, ring, lane, j, start):
        dev = rx_axis(h, ring)(1 if j % 2 == 0 else -1)
        if start:
            send(src, dst, rx_ss.at[h, lane, j], rx_rs.at[h, lane, j], dev)
        else:
            got(dst, rx_ss.at[h, lane, j], rx_rs.at[h, lane, j], dev)

    ORDER = (2, 1, 3, 0)
    for o2 in ORDER:
        for h in (0, 1):
            for j in (0, 1):
                xs1[h, o2, 0, 16 * j : 16 * j + 16] = q(h, 2, o2, j).astype(BF)
                rx(xs1.at[h, o2, 0, 16 * j : 16 * j + 16], xr1h.at[h, o2, j], h, 0, o2, j, True)

    def w1_wait(i, _):
        w1_copy(i, r, (r + 16 - i) % 16).wait_recv()
        return 0

    lax.fori_loop(1, 16, w1_wait, 0)
    total = wr[0].astype(F32)
    for i in range(1, 16):
        total = total + wr[i].astype(F32)
    wz[c] = total.astype(BF)

    def w2_copy(i, peer, mine):
        return rc(wz.at[mine], wz.at[mine], w2_ss.at[i], w2_rs.at[i], (r, peer))

    def w2_send(i, _):
        w2_copy(i, (c + i) % 16, c).start()
        return 0

    lax.fori_loop(1, 16, w2_send, 0)

    for o2 in ORDER:
        for h in (0, 1):
            for j, o in ((0, 1), (1, 3)):
                rx(None, xr1h.at[h, o2, j], h, 0, o2, j, False)
                xs1[h, o2, 1 + j, 16 * j : 16 * j + 16] = (q(h, o, o2, j) + xr1h[h, o2, j].astype(F32)).astype(BF)
                xs1[h, o2, 1 + j, 16 - 16 * j : 32 - 16 * j] = q(h, o, o2, 1 - j).astype(BF)
                rx(xs1.at[h, o2, 1 + j], xr1f.at[h, o2, j], h, 0, o2, 2 + j, True)

    for o2 in ORDER:
        for h in (0, 1):
            for j in (0, 1):
                rx(None, xr1f.at[h, o2, j], h, 0, o2, 2 + j, False)
            s1[h, o2] = q(h, 0, o2, None) + xr1f[h, o2, 0].astype(F32) + xr1f[h, o2, 1].astype(F32)
            if o2 == 2:
                for j in (0, 1):
                    xs2[h, 0, 16 * j : 16 * j + 16] = s1[h, 2, 16 * j : 16 * j + 16].astype(BF)
                    rx(xs2.at[h, 0, 16 * j : 16 * j + 16], xr2h.at[h, j], h, 1, 4, j, True)

    def w2_wait(i, _):
        w2_copy(i, c, (c + 16 - i) % 16).wait_recv()
        return 0

    lax.fori_loop(1, 16, w2_wait, 0)
    total = wz[0].astype(F32)
    for i in range(1, 16):
        total = total + wz[i].astype(F32)
    wg_ref[w_rows(r)] = total.astype(BF)

    def w3_copy(i, peer, mine):
        return rc(wg_ref.at[w_rows(mine)], wg_ref.at[w_rows(mine)], w3_ss.at[i], w3_rs.at[i], (peer, c))

    def w3_send(i, _):
        w3_copy(i, (r + i) % 16, r).start()
        return 0

    lax.fori_loop(1, 16, w3_send, 0)

    for h in (0, 1):
        for j, o in ((0, 1), (1, 3)):
            rx(None, xr2h.at[h, j], h, 1, 4, j, False)
            xs2[h, 1 + j, 16 * j : 16 * j + 16] = (s1[h, o, 16 * j : 16 * j + 16] + xr2h[h, j].astype(F32)).astype(BF)
            xs2[h, 1 + j, 16 - 16 * j : 32 - 16 * j] = s1[h, o, 16 - 16 * j : 32 - 16 * j].astype(BF)
            rx(xs2.at[h, 1 + j], xr2f.at[h, j], h, 1, 4, 2 + j, True)
    for h in (0, 1):
        for j in (0, 1):
            rx(None, xr2f.at[h, j], h, 1, 4, 2 + j, False)
        value = s1[h, 0] + xr2f[h, 0].astype(F32) + xr2f[h, 1].astype(F32)
        fg_ref[:, h * 1024 : (h + 1) * 1024] = value.astype(BF)

    def last(i, _):
        act_copy(i, c, (c + 16 - i) % 16).wait_recv()
        w3_copy(i, r, (r + 16 - i) % 16).wait_recv()
        act_copy(i, (c + i) % 16, c).wait_send()
        cot_copy(i, (c + i) % 16, c).wait_send()
        w1_copy(i, (r + i) % 16, r).wait_send()
        w2_copy(i, (c + i) % 16, c).wait_send()
        w3_copy(i, (r + i) % 16, r).wait_send()
        return 0

    lax.fori_loop(1, 16, last, 0)
    for copy in sent:
        copy.wait_send()


def layer(xt, cot, weight, a):
    dma = pltpu.SemaphoreType.DMA
    vm = pltpu.VMEM
    vspec = pl.BlockSpec(memory_space=pltpu.VMEM)
    return pl.pallas_call(
        layer_kernel,
        out_shape=(
            jax.ShapeDtypeStruct((32, 2048), BF),
            jax.ShapeDtypeStruct((32, 2048), BF),
            jax.ShapeDtypeStruct((512, 512), BF),
        ),
        in_specs=[vspec] * 3 + [pl.BlockSpec(memory_space=pl.ANY)],
        out_specs=(vspec,) * 3,
        scratch_shapes=[
            vm((2048, 2048), BF),
            vm((2, 4, 4, 32, 1024), BF),
            vm((512, 128), BF),
            vm((8, 512, 128), F32),
            vm((8, 512, 128), BF),
            vm((8, 512, 128), BF),
            vm((2, 4, 512, 128), BF),
            vm((2, 5, 512, 128), BF),
            vm((512, 128), BF),
            vm((512, 128), BF),
            vm((512, 128), BF),
            vm((8, 2, 512, 128), BF),
            vm((512, 2048), F32),
            vm((2, 4, 3, 32, 1024), BF),
            vm((2, 4, 2, 16, 1024), BF),
            vm((2, 4, 2, 32, 1024), BF),
            vm((2, 4, 32, 1024), F32),
            vm((2, 3, 32, 1024), BF),
            vm((2, 2, 16, 1024), BF),
            vm((2, 2, 32, 1024), BF),
            vm((512, 512), BF),
            vm((16, 32, 512), BF),
            vm((16, 32, 512), BF),
            dma,
            dma,
        ]
        + [dma((16,))] * 2
        + [dma((2, 5, 4))] * 2
        + [dma((8,))] * 2
        + [dma((2, 5, NS))] * 2
        + [dma((16,))] * 2
        + [dma((2, 4, NS))] * 2
        + [dma((8,))] * 2
        + [dma((2, 5, 4))] * 2
        + [dma((16,))] * 6,
        compiler_params=pltpu.CompilerParams(
            collective_id=0, has_side_effects=True, vmem_limit_bytes=56 << 20
        ),
        name="layer",
    )(xt, cot, weight, a)


def shards(features, weight, block_cols, block_count, edge_src, edge_dst, edge_weight, cotangent):
    a = build(block_cols[:, 0, :], block_count[:, 0], edge_src[:, 0], edge_dst[:, 0], edge_weight[:, 0])
    act, fg, wg = layer(features.T, cotangent.T, weight, a)
    return act.T, fg.T, wg.astype(F32)


def solution(mesh):
    return jax.shard_map(
        shards,
        mesh=mesh,
        in_specs=(
            P("col", "row"),
            P(),
            P("row", "col", None),
            P("row", "col"),
            P("row", "col", None, None),
            P("row", "col", None, None),
            P("row", "col", None, None),
            P("row", "col"),
        ),
        out_specs=(P("row", "col"), P("col", "row"), P()),
        check_vma=False,
    )
```

time: 600 us -> 125 us (0.21)
  waiting for transfers between devices: 250 us -> 0 us
  Pallas kernels: 0 us -> 116 us
  local copies, waits for them, and re-layouts: 113 us -> 4.49 us
  blocking collectives: 101 us -> 0 us
  matrix products: 91.9 us -> 0 us
  other arithmetic: 24.8 us -> 2.15 us
  between operations: 13.8 us -> 0.64 us
    pallas_call x0 -> x2, Pallas kernels: none -> 116 us  [the longest x1 96 us: layer(): pl.pallas_call(layer_kernel, out_shape=(jax.ShapeDtypeStruct((32, 2048),...]
    psum x1 -> x0, blocking collectives: 101 us -> none  [shards(): back = lax.psum(term, 'row').astype(jnp.bfloat16)]
    psum x1 -> x0, waiting for transfers between devices: 98.2 us -> none  [shards(): summed = lax.psum(grad_term, 'col')]
    dot_general x37 -> x0, matrix products: 91.9 us -> none  [the longest x16 31.6 us: forward_block(): jnp.einsum('kab,kbf->af', tile_set, picked, preferred_element_type=jnp.fl...]
    all_gather x3 -> x0, waiting for transfers between devices: 87.8 us -> none  [the longest x1 45.6 us: shards(): weight_grad = lax.all_gather(summed, 'row', axis=0, tiled=True)]
    reduce_scatter x1 -> x0, waiting for transfers between devices: 63.5 us -> none  [shards(): lax.psum_scatter(partial_rows, 'col', scatter_dimension=1, tiled=True)]
    gather x16 -> x0, local copies, waits for them, and re-layouts: 35.3 us -> none  [forward_block(): picked = proj_blocks[index]]
    unnamed x11 -> x2, local copies, waits for them, and re-layouts: 34.1 us -> 3.13 us
  transfers between devices with their start and end apart: 5 -> 0, of which waited for: 4 -> 0; matrix products, arithmetic and copies ran while one was open for 13% -> 0% of each run, Pallas kernels for 0% -> 0%
where the time goes in v1:
time: 125 us; the launch traced here: 123 us
  Pallas kernels  116 us (93%)
  local copies, waits for them, and re-layouts  4.49 us (4%)
  other arithmetic  2.15 us (2%)
    pallas_call x1, Pallas kernels, layer(): pl.pallas_call(layer_kernel, out_shape=(jax.ShapeDtypeStruct((32, 2048),...  96 us
    pallas_call x1, Pallas kernels, build(): pl.pallas_call(build_kernel, out_shape=jax.ShapeDtypeStruct((2048, 2048),...  20 us
    unnamed x2, local copies, waits for them, and re-layouts  3.13 us

profile of v1, /device:TPU:1, one launch (start us, length us, event | category | flops | bytes accessed | tf_op | source)
XLA Modules:
  0.0 123.4 jit_solution(17422778090969138049)
XLA Ops:
  0.6 1.4 %copy.11.cols_ref = s32[16,8]{1,0:T(8,128)} copy(s32[16,8]{0,1:T(8,128)} %bitcast.16) | data formatting | bytes 1024 | tf_op jit(solution)/shard_map/squeeze | solution.py:503
  2.0 20.0 %build.1.a_hbm = bf16[2048,2048]{1,0:T(8,128)(2,1)} custom-call(s32[16,8]{1,0:T(8,128)} %copy.11.cols_ref, s32[16]{0:T(128)} %bitcast.17, s32[16,8,512]{2,1,0:T(8,128)} %bitcast.9, s32[16,8,512]{2,1,0:T(8,128)} %bitcast.10, bf16[16,8,512]{2,1,0:T(8,128)(2,1)} %bitcast.11), custom_call_target="tpu_custom_call" | custom-call | tf_op jit(solution)/shard_map/build/pallas_call | solution.py:43
  22.0 96.0 %layer.1 = (bf16[32,2048]{1,0:T(8,128)(2,1)}, bf16[32,2048]{1,0:T(8,128)(2,1)}, bf16[512,512]{1,0:T(8,128)(2,1)}) custom-call(bf16[32,2048]{1,0:T(8,128)(2,1)} %bitcast.12, bf16[32,2048]{1,0:T(8,128)(2,1)} %bitcast.13, bf16[512,512]{1,0:T(8,128)(2,1)} %w_ref.1, bf16[2048,2048]{1,0:T(8,128)(2,1)} %build.1.a_hbm), custom_call_target="tpu_custom_call" | custom-call | tf_op jit(solution)/shard_map/layer/pallas_call | solution.py:450
  118.1 2.1 %convert_element_type.3 = f32[512,512]{1,0:T(8,128)} convert(bf16[512,512]{1,0:T(8,128)(2,1)} %get-tuple-element.8) | non-fusion elementwise | flops 262144 | bytes 1572864 | tf_op jit(solution)/shard_map/convert_element_type | solution.py:505
  120.2 1.6 %copy.14 = bf16[2048,32]{0,1:T(8,128)(2,1)} copy(bf16[2048,32]{0,1:T(8,128)(2,1)} %bitcast.15) | data formatting | bytes 262144
  121.8 1.6 %copy.15 = bf16[2048,32]{0,1:T(8,128)(2,1)} copy(bf16[2048,32]{0,1:T(8,128)(2,1)} %bitcast.14) | data formatting | bytes 262144

commit v2 on v1

--- a/solution.py
+++ b/solution.py
@@ -14,52 +14,12 @@
 SUB = 512 // NS
 
 
-def build_kernel(cols_ref, counts_ref, src_ref, dst_ref, w_ref, out_ref):
-    g = pl.program_id(0)
-    out_ref[...] = jnp.zeros_like(out_ref)
-    spots = lax.broadcasted_iota(jnp.int32, (128, 512), 0).astype(F32).astype(BF)
-    src = src_ref[0].astype(F32)
-    dst = dst_ref[0].astype(F32)
-    wts = w_ref[0].astype(F32)
-    one = jnp.ones((128, 512), BF)
-    zero = jnp.zeros((128, 512), BF)
-
-    def spread(row):
-        piece = jnp.broadcast_to(row, (16, 512)).astype(BF)
-        return jnp.concatenate([piece] * 8, axis=0)
-
-    for k in range(8):
-
-        @pl.when(k < counts_ref[g])
-        def _():
-            left = jnp.where(spots == spread(dst[k : k + 1]), spread(wts[k : k + 1]), zero)
-            right = jnp.where(spots == spread(src[k : k + 1]), one, zero)
-            tile = lax.dot_general(left, right, NT, preferred_element_type=F32).astype(BF)
-            where = pl.ds(pl.multiple_of(cols_ref[g, k] * 128, 128), 128)
-            out_ref[:, where] = out_ref[:, where] + tile
-
-
-def build(cols, counts, src, dst, wts):
-    return pl.pallas_call(
-        build_kernel,
-        out_shape=jax.ShapeDtypeStruct((2048, 2048), BF),
-        grid_spec=pltpu.PrefetchScalarGridSpec(
-            num_scalar_prefetch=2,
-            grid=(16,),
-            in_specs=[pl.BlockSpec((1, 8, 512), lambda g, *_: (g, 0, 0))] * 3,
-            out_specs=pl.BlockSpec((128, 2048), lambda g, *_: (g, 0)),
-        ),
-        name="build",
-    )(cols, counts, src, dst, wts)
-
-
 def layer_kernel(
-    xt_ref, cot_ref, w_ref, a_hbm,
+    cols_ref, counts_ref, src_ref, dst_ref, ew_ref, xt_ref, cot_ref, w_ref,
     act_ref, fg_ref, wg_ref,
-    a, xg, cotb, pown, psend, precv, zr, zs, axb, actb, slb, tg, acc,
+    a, tiles, xg, cotb, pown, psend, precv, zr, zs, axb, axl, actb, slb, tg, acc,
     xs1, xr1h, xr1f, s1, xs2, xr2h, xr2f,
     wp, wr, wz,
-    a_sem, loc_sem,
     cot_ss, cot_rs, ag_ss, ag_rs, core_ss, core_rs, rz_ss, rz_rs,
     act_ss, act_rs, gz_ss, gz_rs, gc_ss, gc_rs, rx_ss, rx_rs,
     w1_ss, w1_rs, w2_ss, w2_rs, w3_ss, w3_rs,
@@ -103,11 +63,46 @@
         return 0
 
     lax.fori_loop(1, 16, greet, 0)
-    a_copy = pltpu.make_async_copy(a_hbm, a, a_sem)
-    a_copy.start()
     for h in (0, 1):
         xg[h, x, y] = xt_ref[:, h * 1024 : (h + 1) * 1024]
     pl.semaphore_wait(barrier, 30)
+
+    spots = lax.broadcasted_iota(jnp.int32, (128, 512), 0).astype(F32).astype(BF)
+    slots = lax.broadcasted_iota(jnp.int32, (8, 512), 0)
+
+    def spread(row):
+        piece = jnp.broadcast_to(row, (16, row.shape[1])).astype(BF)
+        return jnp.concatenate([piece] * 8, axis=0)
+
+    def build_block(g):
+        src = src_ref[g].astype(F32)
+        dst = dst_ref[g].astype(F32)
+        wts = jnp.where(slots < counts_ref[0, g], ew_ref[g].astype(F32), 0.0)
+        for s in range(8):
+            left = jnp.where(spots == spread(dst[s : s + 1]), spread(wts[s : s + 1]), BF(0))
+            right = jnp.where(spots == spread(src[s : s + 1]), BF(1), BF(0))
+            tiles[s] = lax.dot_general(left, right, NT, preferred_element_type=F32).astype(BF)
+        names = [spread(jnp.full((1, 128), cols_ref[s, g].astype(F32), F32)) for s in range(8)]
+        rows = pl.ds(pl.multiple_of(g * 128, 128), 128)
+
+        def place(j, _):
+            here = spread(jnp.full((1, 128), j.astype(F32), F32))
+            total = jnp.where(names[0] == here, tiles[0], BF(0))
+            for s in range(1, 8):
+                total = total + jnp.where(names[s] == here, tiles[s], BF(0))
+            a[rows, pl.ds(pl.multiple_of(j * 128, 128), 128)] = total
+            return 0
+
+        lax.fori_loop(0, 16, place, 0, unroll=4)
+
+    def build(*offsets):
+        for d in offsets:
+
+            def one(i, _, d=d):
+                build_block((z + d) % 8 * 2 + i)
+                return 0
+
+            lax.fori_loop(0, 2, one, 0)
 
     def xg_at(h, o1, o2):
         if h == 0:
@@ -162,25 +157,31 @@
     lax.fori_loop(1, 16, cot_send, 0)
     cotb[pl.ds(pl.multiple_of(c * 32, 32), 32), :] = cot_ref[:, pl.ds(pl.multiple_of(c * 128, 128), 128)]
 
+    build(4)
     for j, o in ((0, 3), (1, 1)):
         for h in (0, 1):
             ag_got(h, 0, 0, j, xg_at(h, o, 0))
             ag_send(h, 0, 0, 2 + j, xg_at(h, o, 0))
             ag_ring2_own(h, o)
+    build(3)
     for h in (0, 1):
         ag_ring2_pass(h, 0)
     for h in (0, 1):
         for j in (2, 3):
             ag_got(h, 0, 0, j, xg_at(h, 2, 0))
         ag_ring2_own(h, 2)
-    for o1 in (3, 1, 2):
+    build(5)
+    for o1 in (3, 1):
         for h in (0, 1):
             ag_ring2_pass(h, o1)
+    build(2)
+    for h in (0, 1):
+        ag_ring2_pass(h, 2)
+    build(6)
     for o1 in (0, 3, 1, 2):
         for h in (0, 1):
             for j in (2, 3):
                 ag_got(h, 1, 1 + o1, j, xg_at(h, o1, 2))
-    a_copy.wait()
 
     def product(d):
         rows = pl.ds(pl.multiple_of((z + d) % 8 * 256, 256), 256)
@@ -192,7 +193,7 @@
         low, high = total[:, 0:128], total[:, 128:256]
         first = k == 0
         pown[d] = jnp.where(first, low, high)
-        psend[d] = jnp.where(first, high, low).astype(BF)
+        psend[d] = jnp.where(first, high, low)
         send(psend.at[d], precv.at[d], core_ss.at[d], core_rs.at[d], twin)
 
     def twin_got(d):
@@ -211,7 +212,7 @@
                 if not z_rows(side, dist, j):
                     continue
                 d = dist if side == 0 else (8 - dist) % 8
-                value = pown[d, rows] + precv[d, rows].astype(F32)
+                value = pown[d, rows] + precv[d, rows]
                 if dist < 4 and z_rows(side, dist + 1, j):
                     got(zr.at[side, dist, rows], rz_ss.at[side, dist + 1, j], rz_rs.at[side, dist + 1, j], at_z(-1 if side == 0 else 1))
                     value = value + zr[side, dist, rows].astype(F32)
@@ -228,19 +229,23 @@
     product(2)
     product(6)
     z_step(3)
+    build(1)
     product(1)
+    build(7)
     product(7)
     z_step(2)
+    build(0)
     product(0)
     z_step(1)
     twin_got(0)
     for j in range(NS):
         rows = pl.ds(j * SUB, SUB)
-        value = pown[0, rows] + precv[0, rows].astype(F32)
+        value = pown[0, rows] + precv[0, rows]
         for side in (0, 1):
             got(zr.at[side, 0, rows], rz_ss.at[side, 1, j], rz_rs.at[side, 1, j], at_z(-1 if side == 0 else 1))
             value = value + zr[side, 0, rows].astype(F32)
         axb[rows] = value.astype(BF)
+        axl[rows] = (value - axb[rows].astype(F32)).astype(BF)
 
     def cot_wait(i, _):
         cot_copy(i, c, (c + 16 - i) % 16).wait_recv()
@@ -248,6 +253,7 @@
 
     lax.fori_loop(1, 16, cot_wait, 0)
     hidden = lax.dot_general(w_ref[...], axb[...], TN, preferred_element_type=F32)
+    hidden = hidden + lax.dot_general(w_ref[...], axl[...], TN, preferred_element_type=F32)
     sig = jax.nn.sigmoid(hidden)
     actb[...] = (hidden * sig).astype(BF)
     slb[...] = (cotb[...].astype(F32) * sig * (1.0 + hidden * (1.0 - sig))).astype(BF)
@@ -394,7 +400,7 @@
             s1[h, o2] = q(h, 0, o2, None) + xr1f[h, o2, 0].astype(F32) + xr1f[h, o2, 1].astype(F32)
             if o2 == 2:
                 for j in (0, 1):
-                    xs2[h, 0, 16 * j : 16 * j + 16] = s1[h, 2, 16 * j : 16 * j + 16].astype(BF)
+                    xs2[h, 0, 16 * j : 16 * j + 16] = s1[h, 2, 16 * j : 16 * j + 16]
                     rx(xs2.at[h, 0, 16 * j : 16 * j + 16], xr2h.at[h, j], h, 1, 4, j, True)
 
     def w2_wait(i, _):
@@ -419,13 +425,13 @@
     for h in (0, 1):
         for j, o in ((0, 1), (1, 3)):
             rx(None, xr2h.at[h, j], h, 1, 4, j, False)
-            xs2[h, 1 + j, 16 * j : 16 * j + 16] = (s1[h, o, 16 * j : 16 * j + 16] + xr2h[h, j].astype(F32)).astype(BF)
-            xs2[h, 1 + j, 16 - 16 * j : 32 - 16 * j] = s1[h, o, 16 - 16 * j : 32 - 16 * j].astype(BF)
+            xs2[h, 1 + j, 16 * j : 16 * j + 16] = (s1[h, o, 16 * j : 16 * j + 16] + xr2h[h, j])
+            xs2[h, 1 + j, 16 - 16 * j : 32 - 16 * j] = s1[h, o, 16 - 16 * j : 32 - 16 * j]
             rx(xs2.at[h, 1 + j], xr2f.at[h, j], h, 1, 4, 2 + j, True)
     for h in (0, 1):
         for j in (0, 1):
             rx(None, xr2f.at[h, j], h, 1, 4, 2 + j, False)
-        value = s1[h, 0] + xr2f[h, 0].astype(F32) + xr2f[h, 1].astype(F32)
+        value = s1[h, 0] + xr2f[h, 0] + xr2f[h, 1]
         fg_ref[:, h * 1024 : (h + 1) * 1024] = value.astype(BF)
 
     def last(i, _):
@@ -443,7 +449,7 @@
         copy.wait_send()
 
 
-def layer(xt, cot, weight, a):
+def layer(cols, counts, src, dst, ew, xt, cot, weight):
     dma = pltpu.SemaphoreType.DMA
     vm = pltpu.VMEM
     vspec = pl.BlockSpec(memory_space=pltpu.VMEM)
@@ -454,17 +460,19 @@
             jax.ShapeDtypeStruct((32, 2048), BF),
             jax.ShapeDtypeStruct((512, 512), BF),
         ),
-        in_specs=[vspec] * 3 + [pl.BlockSpec(memory_space=pl.ANY)],
+        in_specs=[pl.BlockSpec(memory_space=pltpu.SMEM)] * 2 + [vspec] * 6,
         out_specs=(vspec,) * 3,
         scratch_shapes=[
             vm((2048, 2048), BF),
+            vm((8, 128, 128), BF),
             vm((2, 4, 4, 32, 1024), BF),
             vm((512, 128), BF),
             vm((8, 512, 128), F32),
-            vm((8, 512, 128), BF),
-            vm((8, 512, 128), BF),
+            vm((8, 512, 128), F32),
+            vm((8, 512, 128), F32),
             vm((2, 4, 512, 128), BF),
             vm((2, 5, 512, 128), BF),
+            vm((512, 128), BF),
             vm((512, 128), BF),
             vm((512, 128), BF),
             vm((512, 128), BF),
@@ -474,14 +482,12 @@
             vm((2, 4, 2, 16, 1024), BF),
             vm((2, 4, 2, 32, 1024), BF),
             vm((2, 4, 32, 1024), F32),
-            vm((2, 3, 32, 1024), BF),
-            vm((2, 2, 16, 1024), BF),
-            vm((2, 2, 32, 1024), BF),
+            vm((2, 3, 32, 1024), F32),
+            vm((2, 2, 16, 1024), F32),
+            vm((2, 2, 32, 1024), F32),
             vm((512, 512), BF),
             vm((16, 32, 512), BF),
             vm((16, 32, 512), BF),
-            dma,
-            dma,
         ]
         + [dma((16,))] * 2
         + [dma((2, 5, 4))] * 2
@@ -493,16 +499,50 @@
         + [dma((2, 5, 4))] * 2
         + [dma((16,))] * 6,
         compiler_params=pltpu.CompilerParams(
-            collective_id=0, has_side_effects=True, vmem_limit_bytes=56 << 20
+            collective_id=0, has_side_effects=True, vmem_limit_bytes=58 << 20
         ),
         name="layer",
-    )(xt, cot, weight, a)
+    )(cols, counts, src, dst, ew, xt, cot, weight)
+
+
+def finish_kernel(act_ref, fg_ref, wg_ref, act_out, fg_out, wg_out, wg_in, sems):
+    copies = [
+        pltpu.make_async_copy(wg_ref, wg_in, sems.at[0]),
+        pltpu.make_async_copy(act_ref, act_out, sems.at[1]),
+        pltpu.make_async_copy(fg_ref, fg_out, sems.at[2]),
+    ]
+    for copy in copies:
+        copy.start()
+    copies[0].wait()
+    wg_out[...] = wg_in[...].astype(F32)
+    copies[1].wait()
+    copies[2].wait()
+
+
+def finish(act, fg, wg):
+    anywhere = pl.BlockSpec(memory_space=pl.ANY)
+    return pl.pallas_call(
+        finish_kernel,
+        out_shape=(
+            jax.ShapeDtypeStruct((32, 2048), BF),
+            jax.ShapeDtypeStruct((32, 2048), BF),
+            jax.ShapeDtypeStruct((512, 512), F32),
+        ),
+        in_specs=[anywhere] * 3,
+        out_specs=(anywhere, anywhere, pl.BlockSpec(memory_space=pltpu.VMEM)),
+        scratch_shapes=[pltpu.VMEM((512, 512), BF), pltpu.SemaphoreType.DMA((3,))],
+        compiler_params=pltpu.CompilerParams(vmem_limit_bytes=58 << 20),
+        name="finish",
+    )(act, fg, wg)
 
 
 def shards(features, weight, block_cols, block_count, edge_src, edge_dst, edge_weight, cotangent):
-    a = build(block_cols[:, 0, :], block_count[:, 0], edge_src[:, 0], edge_dst[:, 0], edge_weight[:, 0])
-    act, fg, wg = layer(features.T, cotangent.T, weight, a)
-    return act.T, fg.T, wg.astype(F32)
+    outs = layer(
+        block_cols[:, 0, :].T, block_count.T, edge_src[:, 0], edge_dst[:, 0], edge_weight[:, 0],
+        features.T, cotangent.T, weight,
+    )
+    act, fg, wg = finish(*outs)
+    return act.T, fg.T, wg
 
 
 def solution(mesh):

time: 125 us -> 109 us (0.87); the launches traced: 123 us -> 109 us
  Pallas kernels: 116 us -> 108 us
  local copies, waits for them, and re-layouts: 4.49 us -> 0 us
  other arithmetic: 2.15 us -> 0 us
    pallas_call x1, Pallas kernels: 20 us -> 10 us  [finish(): pl.pallas_call(finish_kernel, out_shape=(jax.ShapeDtypeStruct((32, 2048),...]
    unnamed x2 -> x0, local copies, waits for them, and re-layouts: 3.13 us -> none
    pallas_call x1, Pallas kernels: 96 us -> 98.3 us  [layer(): pl.pallas_call(layer_kernel, out_shape=(jax.ShapeDtypeStruct((32, 2048),...]
    convert_element_type x1 -> x0, other arithmetic: 2.15 us -> none  [shards(): return (act.T, fg.T, wg.astype(F32))]
    squeeze x1 -> x0, local copies, waits for them, and re-layouts: 1.36 us -> none  [shards(): block_cols[:, 0, :]]
where the time goes in v2:
time: 109 us
  Pallas kernels  108 us (99%)
    pallas_call x1, Pallas kernels, layer(): pl.pallas_call(layer_kernel, out_shape=(jax.ShapeDtypeStruct((32, 2048),...  98.3 us
    pallas_call x1, Pallas kernels, finish(): pl.pallas_call(finish_kernel, out_shape=(jax.ShapeDtypeStruct((32, 2048),...  10 us

profile of v2, /device:TPU:1, one launch (start us, length us, event | category | flops | bytes accessed | tf_op | source)
XLA Modules:
  0.0 109.2 jit_solution(17953042131549628150)
XLA Ops:
  0.6 98.3 %layer.1 = (bf16[32,2048]{1,0:T(8,128)(2,1)}, bf16[32,2048]{1,0:T(8,128)(2,1)}, bf16[512,512]{1,0:T(8,128)(2,1)}) custom-call(s32[8,16]{1,0:T(8,128)} %bitcast.16, s32[1,16]{1,0:T(1,128)} %bitcast.17, s32[16,8,512]{2,1,0:T(8,128)} %bitcast.11, s32[16,8,512]{2,1,0:T(8,128)} %bitcast.12, bf16[16,8,512]{2,1,0:T(8,128)(2,1)} %bitcast.13, ...), custom_call_target="tpu_custom_call" | custom-call | tf_op jit(solution)/shard_map/layer/pallas_call | solution.py:456
  99.0 10.0 %finish.1 = (bf16[32,2048]{1,0:T(8,128)(2,1)}, bf16[32,2048]{1,0:T(8,128)(2,1)}, f32[512,512]{1,0:T(8,128)}) custom-call(bf16[32,2048]{1,0:T(8,128)(2,1)} %get-tuple-element.9.act_ref, bf16[32,2048]{1,0:T(8,128)(2,1)} %get-tuple-element.10.fg_ref, bf16[512,512]{1,0:T(8,128)(2,1)} %get-tuple-element.11.wg_ref), custom_call_target="tpu_custom_call" | custom-call | tf_op jit(solution)/shard_map/finish/pallas_call | solution.py:524

commit v3 on v2

--- a/solution.py
+++ b/solution.py
@@ -10,19 +10,19 @@
 F32 = jnp.float32
 NT = (((1,), (1,)), ((), ()))
 TN = (((0,), (0,)), ((), ()))
-NS = 2
+NS = 4
 SUB = 512 // NS
 
 
 def layer_kernel(
     cols_ref, counts_ref, src_ref, dst_ref, ew_ref, xt_ref, cot_ref, w_ref,
     act_ref, fg_ref, wg_ref,
-    a, tiles, xg, cotb, pown, psend, precv, zr, zs, axb, axl, actb, slb, tg, acc,
+    a, tiles, xg, cotb, pown, psend, precv, zr, zs, axb, axl, actb, slb, sll, tg, acc,
     xs1, xr1h, xr1f, s1, xs2, xr2h, xr2f,
-    wp, wr, wz,
+    wp, w0r, w0s, w1r, wz,
     cot_ss, cot_rs, ag_ss, ag_rs, core_ss, core_rs, rz_ss, rz_rs,
     act_ss, act_rs, gz_ss, gz_rs, gc_ss, gc_rs, rx_ss, rx_rs,
-    w1_ss, w1_rs, w2_ss, w2_rs, w3_ss, w3_rs,
+    w0_ss, w0_rs, w1_ss, w1_rs, w2_ss, w2_rs, w3_ss, w3_rs,
 ):
     r = lax.axis_index("row")
     c = lax.axis_index("col")
@@ -64,7 +64,8 @@
 
     lax.fori_loop(1, 16, greet, 0)
     for h in (0, 1):
-        xg[h, x, y] = xt_ref[:, h * 1024 : (h + 1) * 1024]
+        for b in range(h * 8, h * 8 + 8):
+            xg[b, x, y] = xt_ref[:, b * 128 : (b + 1) * 128]
     pl.semaphore_wait(barrier, 30)
 
     spots = lax.broadcasted_iota(jnp.int32, (128, 512), 0).astype(F32).astype(BF)
@@ -74,40 +75,51 @@
         piece = jnp.broadcast_to(row, (16, row.shape[1])).astype(BF)
         return jnp.concatenate([piece] * 8, axis=0)
 
-    def build_block(g):
+    def make_block(g):
         src = src_ref[g].astype(F32)
         dst = dst_ref[g].astype(F32)
         wts = jnp.where(slots < counts_ref[0, g], ew_ref[g].astype(F32), 0.0)
         for s in range(8):
             left = jnp.where(spots == spread(dst[s : s + 1]), spread(wts[s : s + 1]), BF(0))
             right = jnp.where(spots == spread(src[s : s + 1]), BF(1), BF(0))
-            tiles[s] = lax.dot_general(left, right, NT, preferred_element_type=F32).astype(BF)
+            tile = lax.dot_general(left, right, NT, preferred_element_type=F32)
+            tiles[g, :, s * 128 : (s + 1) * 128] = tile.astype(BF)
+
+    def place_block(g):
         names = [spread(jnp.full((1, 128), cols_ref[s, g].astype(F32), F32)) for s in range(8)]
         rows = pl.ds(pl.multiple_of(g * 128, 128), 128)
-
-        def place(j, _):
-            here = spread(jnp.full((1, 128), j.astype(F32), F32))
-            total = jnp.where(names[0] == here, tiles[0], BF(0))
-            for s in range(1, 8):
-                total = total + jnp.where(names[s] == here, tiles[s], BF(0))
-            a[rows, pl.ds(pl.multiple_of(j * 128, 128), 128)] = total
+        for j in range(16):
+            here = BF(j)
+            t = [
+                jnp.where(names[s] == here, tiles[g, :, s * 128 : (s + 1) * 128], BF(0))
+                for s in range(8)
+            ]
+            total = ((t[0] + t[1]) + (t[2] + t[3])) + ((t[4] + t[5]) + (t[6] + t[7]))
+            a[rows, j * 128 : (j + 1) * 128] = total
+
+    def nth_block(i):
+        n = i // 2
+        step = (n + 1) // 2
+        d = 4 + jnp.where(n % 2 == 1, -step, step)
+        return (z + d) % 8 * 2 + i % 2
+
+    def over(which, start, stop):
+        def one(i, _):
+            which(nth_block(i))
             return 0
 
-        lax.fori_loop(0, 16, place, 0, unroll=4)
-
-    def build(*offsets):
-        for d in offsets:
-
-            def one(i, _, d=d):
-                build_block((z + d) % 8 * 2 + i)
-                return 0
-
-            lax.fori_loop(0, 2, one, 0)
+        lax.fori_loop(start, stop, one, 0)
+
+    def make(start, stop):
+        over(make_block, start, stop)
+
+    def place(start, stop):
+        over(place_block, start, stop)
 
     def xg_at(h, o1, o2):
         if h == 0:
-            return xg.at[0, (x + o2) % 4, (y + o1) % 4]
-        return xg.at[1, (x + o1) % 4, (y + o2) % 4]
+            return xg.at[0:8, (x + o2) % 4, (y + o1) % 4]
+        return xg.at[8:16, (x + o1) % 4, (y + o2) % 4]
 
     def axis(h, ring):
         return (at_y, at_x)[(h + ring) % 2]
@@ -115,17 +127,17 @@
     def ag_send(h, ring, lane, j, piece):
         dev = axis(h, ring)(1 if j % 2 == 0 else -1)
         if j == 2:
-            piece = piece.at[0:16]
+            piece = piece.at[:, 0:16]
         if j == 3:
-            piece = piece.at[16:32]
+            piece = piece.at[:, 16:32]
         send(piece, piece, ag_ss.at[h, lane, j], ag_rs.at[h, lane, j], dev)
 
     def ag_got(h, ring, lane, j, piece):
         dev = axis(h, ring)(-1 if j % 2 == 0 else 1)
         if j == 2:
-            piece = piece.at[0:16]
+            piece = piece.at[:, 0:16]
         if j == 3:
-            piece = piece.at[16:32]
+            piece = piece.at[:, 16:32]
         got(piece, ag_ss.at[h, lane, j], ag_rs.at[h, lane, j], dev)
 
     def ag_ring2_own(h, o1):
@@ -157,44 +169,44 @@
     lax.fori_loop(1, 16, cot_send, 0)
     cotb[pl.ds(pl.multiple_of(c * 32, 32), 32), :] = cot_ref[:, pl.ds(pl.multiple_of(c * 128, 128), 128)]
 
-    build(4)
+    make(0, 3)
     for j, o in ((0, 3), (1, 1)):
         for h in (0, 1):
             ag_got(h, 0, 0, j, xg_at(h, o, 0))
             ag_send(h, 0, 0, 2 + j, xg_at(h, o, 0))
             ag_ring2_own(h, o)
-    build(3)
+    make(3, 6)
     for h in (0, 1):
         ag_ring2_pass(h, 0)
     for h in (0, 1):
         for j in (2, 3):
             ag_got(h, 0, 0, j, xg_at(h, 2, 0))
         ag_ring2_own(h, 2)
-    build(5)
+    make(6, 9)
     for o1 in (3, 1):
         for h in (0, 1):
             ag_ring2_pass(h, o1)
-    build(2)
+    make(9, 12)
     for h in (0, 1):
         ag_ring2_pass(h, 2)
-    build(6)
+    make(12, 16)
     for o1 in (0, 3, 1, 2):
         for h in (0, 1):
             for j in (2, 3):
                 ag_got(h, 1, 1 + o1, j, xg_at(h, o1, 2))
 
+    def block_product(g):
+        picked = []
+        for s in range(8):
+            picked.append(xg[cols_ref[s, g]].reshape(512, 128))
+        left = jnp.concatenate(picked, axis=1)
+        return lax.dot_general(left, tiles[g], NT, preferred_element_type=F32)
+
     def product(d):
-        rows = pl.ds(pl.multiple_of((z + d) % 8 * 256, 256), 256)
-        total = lax.dot_general(
-            xg[0].reshape(512, 1024), a[rows, 0:1024], NT, preferred_element_type=F32
-        ) + lax.dot_general(
-            xg[1].reshape(512, 1024), a[rows, 1024:2048], NT, preferred_element_type=F32
-        )
-        low, high = total[:, 0:128], total[:, 128:256]
-        first = k == 0
-        pown[d] = jnp.where(first, low, high)
-        psend[d] = jnp.where(first, high, low)
+        first = (z + d) % 8 * 2
+        psend[d] = block_product(first + 1 - k)
         send(psend.at[d], precv.at[d], core_ss.at[d], core_rs.at[d], twin)
+        pown[d] = block_product(first + k)
 
     def twin_got(d):
         got(precv.at[d], core_ss.at[d], core_rs.at[d], twin)
@@ -228,15 +240,16 @@
     z_step(4)
     product(2)
     product(6)
+    place(0, 2)
     z_step(3)
-    build(1)
     product(1)
-    build(7)
     product(7)
+    place(2, 5)
     z_step(2)
-    build(0)
     product(0)
+    place(5, 10)
     z_step(1)
+    place(10, 16)
     twin_got(0)
     for j in range(NS):
         rows = pl.ds(j * SUB, SUB)
@@ -256,8 +269,13 @@
     hidden = hidden + lax.dot_general(w_ref[...], axl[...], TN, preferred_element_type=F32)
     sig = jax.nn.sigmoid(hidden)
     actb[...] = (hidden * sig).astype(BF)
-    slb[...] = (cotb[...].astype(F32) * sig * (1.0 + hidden * (1.0 - sig))).astype(BF)
-    tg[z, k] = jnp.dot(w_ref[...], slb[...], preferred_element_type=F32).astype(BF)
+    slope = cotb[...].astype(F32) * sig * (1.0 + hidden * (1.0 - sig))
+    slb[...] = slope.astype(BF)
+    sll[...] = (slope - slb[...].astype(F32)).astype(BF)
+    tg[z, k] = (
+        jnp.dot(w_ref[...], slb[...], preferred_element_type=F32)
+        + jnp.dot(w_ref[...], sll[...], preferred_element_type=F32)
+    ).astype(BF)
 
     def gz_send(side, dist, j):
         owner = (z - dist + 8) % 8 if side == 0 else (z + dist) % 8
@@ -293,23 +311,72 @@
         act_copy(i, (c + i) % 16, c).start()
         return 0
 
-    lax.fori_loop(1, 16, act_send, 0)
-    act_ref[:, pl.ds(pl.multiple_of(c * 128, 128), 128)] = actb[pl.ds(pl.multiple_of(c * 32, 32), 32), :]
-
-    wp[...] = lax.dot_general(axb[...], slb[...], NT, preferred_element_type=F32).astype(BF)
-
-    def w_rows(i):
-        return pl.ds(pl.multiple_of(i * 32, 32), 32)
+    wp[...] = (
+        lax.dot_general(axb[...], slb[...], NT, preferred_element_type=F32)
+        .astype(BF)
+        .reshape(16, 2, 16, 512)
+    )
+    send(wp.at[:, 1 - k], w0r, w0_ss.at[0], w0_rs.at[0], twin)
 
     def w1_copy(i, peer, mine):
-        return rc(wp.at[w_rows(peer)], wr.at[mine], w1_ss.at[i], w1_rs.at[i], (peer, c))
+        return rc(w0s.at[peer], w1r.at[mine], w1_ss.at[i], w1_rs.at[i], (peer, c))
 
     def w1_send(i, _):
         w1_copy(i, (r + i) % 16, r).start()
         return 0
 
-    lax.fori_loop(1, 16, w1_send, 0)
-    wr[r] = wp[w_rows(r)]
+    def w1_wait(i, _):
+        w1_copy(i, r, (r + 16 - i) % 16).wait_recv()
+        return 0
+
+    def w2_copy(i, peer, mine):
+        return rc(wz.at[mine], wz.at[mine], w2_ss.at[i], w2_rs.at[i], (r, peer * 2 + k))
+
+    def w2_send(i, _):
+        w2_copy(i, (z + i) % 8, z).start()
+        return 0
+
+    def w2_wait(i, _):
+        w2_copy(i, z, (z + 8 - i) % 8).wait_recv()
+        return 0
+
+    def w3_copy(i, peer, mine):
+        return rc(wg_ref.at[mine, k], wg_ref.at[mine, k], w3_ss.at[i], w3_rs.at[i], (peer, c))
+
+    def w3_send(i, _):
+        w3_copy(i, (r + i) % 16, r).start()
+        return 0
+
+    def w3_wait(i, _):
+        w3_copy(i, r, (r + 16 - i) % 16).wait_recv()
+        return 0
+
+    def w_start_row():
+        got(w0r, w0_ss.at[0], w0_rs.at[0], twin)
+        w0s[...] = (wp[:, k].astype(F32) + w0r[...].astype(F32)).astype(BF)
+        lax.fori_loop(1, 16, w1_send, 0)
+        w1r[r] = w0s[r]
+
+    def w_start_z():
+        lax.fori_loop(1, 16, w1_wait, 0)
+        total = w1r[0].astype(F32)
+        for i in range(1, 16):
+            total = total + w1r[i].astype(F32)
+        wz[z] = total.astype(BF)
+        lax.fori_loop(1, 8, w2_send, 0)
+
+    def w_start_last():
+        lax.fori_loop(1, 8, w2_wait, 0)
+        total = wz[0].astype(F32)
+        for i in range(1, 8):
+            total = total + wz[i].astype(F32)
+        wg_ref[r, k] = total.astype(BF)
+        lax.fori_loop(1, 16, w3_send, 0)
+
+    def w_finish():
+        lax.fori_loop(1, 16, w3_wait, 0)
+        send(wg_ref.at[:, k], wg_ref.at[:, k], w0_ss.at[1], w0_rs.at[1], twin)
+        got(wg_ref.at[:, 1 - k], w0_ss.at[1], w0_rs.at[1], twin)
 
     def gather_step(dist):
         for j in range(NS):
@@ -330,11 +397,28 @@
 
     gc_got(0)
     acc[...] = back_part(0)
-    for dist in (1, 2, 3, 4):
-        gather_step(dist)
-        for d in (4,) if dist == 4 else (dist, 8 - dist):
+    gather_step(1)
+    w_start_row()
+    gather_step(2)
+    for dist in (1, 2):
+        for d in (dist, 8 - dist):
             gc_got(d)
             acc[...] += back_part(d)
+        gather_step(dist + 2)
+    lax.fori_loop(1, 16, act_send, 0)
+    act_ref[:, pl.ds(pl.multiple_of(c * 128, 128), 128)] = actb[pl.ds(pl.multiple_of(c * 32, 32), 32), :]
+    w_start_z()
+    for d in (3, 5):
+        gc_got(d)
+        acc[...] += back_part(d)
+    gc_got(4)
+
+    def last_part(o):
+        block = (z + 4) % 8
+        feats = pl.ds(pl.multiple_of((x + o) % 4 * 128, 128), 128)
+        left = jnp.concatenate([tg[block, 0, feats], tg[block, 1, feats]], axis=1)
+        rows = pl.ds(pl.multiple_of(block * 256, 256), 256)
+        acc[feats] += jnp.dot(left, a[rows, :], preferred_element_type=F32)
 
     def q_rows(h, o1, o2):
         if h == 0:
@@ -360,91 +444,81 @@
             got(dst, rx_ss.at[h, lane, j], rx_rs.at[h, lane, j], dev)
 
     ORDER = (2, 1, 3, 0)
+
+    def s1_halves(h, o2):
+        for j in (0, 1):
+            xs1[h, o2, 0, 16 * j : 16 * j + 16] = q(h, 2, o2, j).astype(BF)
+            rx(xs1.at[h, o2, 0, 16 * j : 16 * j + 16], xr1h.at[h, o2, j], h, 0, o2, j, True)
+
+    def s1_pass(h, o2, j):
+        o = (1, 3)[j]
+        rx(None, xr1h.at[h, o2, j], h, 0, o2, j, False)
+        xs1[h, o2, 1 + j, 16 * j : 16 * j + 16] = (q(h, o, o2, j) + xr1h[h, o2, j].astype(F32)).astype(BF)
+        xs1[h, o2, 1 + j, 16 - 16 * j : 32 - 16 * j] = q(h, o, o2, 1 - j).astype(BF)
+        rx(xs1.at[h, o2, 1 + j], xr1f.at[h, o2, j], h, 0, o2, 2 + j, True)
+
+    def s1_final(h, o2):
+        for j in (0, 1):
+            rx(None, xr1f.at[h, o2, j], h, 0, o2, 2 + j, False)
+        s1[h, o2] = q(h, 0, o2, None) + xr1f[h, o2, 0].astype(F32) + xr1f[h, o2, 1].astype(F32)
+
+    def s2_halves(h):
+        for j in (0, 1):
+            xs2[h, 0, 16 * j : 16 * j + 16] = s1[h, 2, 16 * j : 16 * j + 16].astype(BF)
+            rx(xs2.at[h, 0, 16 * j : 16 * j + 16], xr2h.at[h, j], h, 1, 4, j, True)
+
+    def s2_pass(h, j):
+        o = (1, 3)[j]
+        rx(None, xr2h.at[h, j], h, 1, 4, j, False)
+        xs2[h, 1 + j, 16 * j : 16 * j + 16] = (s1[h, o, 16 * j : 16 * j + 16] + xr2h[h, j].astype(F32)).astype(BF)
+        xs2[h, 1 + j, 16 - 16 * j : 32 - 16 * j] = s1[h, o, 16 - 16 * j : 32 - 16 * j].astype(BF)
+        rx(xs2.at[h, 1 + j], xr2f.at[h, j], h, 1, 4, 2 + j, True)
+
+    def s2_final(h):
+        for j in (0, 1):
+            rx(None, xr2f.at[h, j], h, 1, 4, 2 + j, False)
+        value = s1[h, 0] + xr2f[h, 0].astype(F32) + xr2f[h, 1].astype(F32)
+        fg_ref[:, h * 1024 : (h + 1) * 1024] = value.astype(BF)
+
+    last_part(2)
+    for o2 in ORDER:
+        s1_halves(0, o2)
+    s1_halves(1, 2)
+    for o in (1, 3, 0):
+        last_part(o)
+        s1_halves(1, o)
     for o2 in ORDER:
         for h in (0, 1):
             for j in (0, 1):
-                xs1[h, o2, 0, 16 * j : 16 * j + 16] = q(h, 2, o2, j).astype(BF)
-                rx(xs1.at[h, o2, 0, 16 * j : 16 * j + 16], xr1h.at[h, o2, j], h, 0, o2, j, True)
-
-    def w1_wait(i, _):
-        w1_copy(i, r, (r + 16 - i) % 16).wait_recv()
-        return 0
-
-    lax.fori_loop(1, 16, w1_wait, 0)
-    total = wr[0].astype(F32)
-    for i in range(1, 16):
-        total = total + wr[i].astype(F32)
-    wz[c] = total.astype(BF)
-
-    def w2_copy(i, peer, mine):
-        return rc(wz.at[mine], wz.at[mine], w2_ss.at[i], w2_rs.at[i], (r, peer))
-
-    def w2_send(i, _):
-        w2_copy(i, (c + i) % 16, c).start()
-        return 0
-
-    lax.fori_loop(1, 16, w2_send, 0)
-
+                s1_pass(h, o2, j)
+    w_start_last()
     for o2 in ORDER:
         for h in (0, 1):
-            for j, o in ((0, 1), (1, 3)):
-                rx(None, xr1h.at[h, o2, j], h, 0, o2, j, False)
-                xs1[h, o2, 1 + j, 16 * j : 16 * j + 16] = (q(h, o, o2, j) + xr1h[h, o2, j].astype(F32)).astype(BF)
-                xs1[h, o2, 1 + j, 16 - 16 * j : 32 - 16 * j] = q(h, o, o2, 1 - j).astype(BF)
-                rx(xs1.at[h, o2, 1 + j], xr1f.at[h, o2, j], h, 0, o2, 2 + j, True)
-
-    for o2 in ORDER:
-        for h in (0, 1):
-            for j in (0, 1):
-                rx(None, xr1f.at[h, o2, j], h, 0, o2, 2 + j, False)
-            s1[h, o2] = q(h, 0, o2, None) + xr1f[h, o2, 0].astype(F32) + xr1f[h, o2, 1].astype(F32)
+            s1_final(h, o2)
             if o2 == 2:
-                for j in (0, 1):
-                    xs2[h, 0, 16 * j : 16 * j + 16] = s1[h, 2, 16 * j : 16 * j + 16]
-                    rx(xs2.at[h, 0, 16 * j : 16 * j + 16], xr2h.at[h, j], h, 1, 4, j, True)
-
-    def w2_wait(i, _):
-        w2_copy(i, c, (c + 16 - i) % 16).wait_recv()
-        return 0
-
-    lax.fori_loop(1, 16, w2_wait, 0)
-    total = wz[0].astype(F32)
-    for i in range(1, 16):
-        total = total + wz[i].astype(F32)
-    wg_ref[w_rows(r)] = total.astype(BF)
-
-    def w3_copy(i, peer, mine):
-        return rc(wg_ref.at[w_rows(mine)], wg_ref.at[w_rows(mine)], w3_ss.at[i], w3_rs.at[i], (peer, c))
-
-    def w3_send(i, _):
-        w3_copy(i, (r + i) % 16, r).start()
-        return 0
-
-    lax.fori_loop(1, 16, w3_send, 0)
-
-    for h in (0, 1):
-        for j, o in ((0, 1), (1, 3)):
-            rx(None, xr2h.at[h, j], h, 1, 4, j, False)
-            xs2[h, 1 + j, 16 * j : 16 * j + 16] = (s1[h, o, 16 * j : 16 * j + 16] + xr2h[h, j])
-            xs2[h, 1 + j, 16 - 16 * j : 32 - 16 * j] = s1[h, o, 16 - 16 * j : 32 - 16 * j]
-            rx(xs2.at[h, 1 + j], xr2f.at[h, j], h, 1, 4, 2 + j, True)
+                s2_halves(h)
     for h in (0, 1):
         for j in (0, 1):
-            rx(None, xr2f.at[h, j], h, 1, 4, 2 + j, False)
-        value = s1[h, 0] + xr2f[h, 0] + xr2f[h, 1]
-        fg_ref[:, h * 1024 : (h + 1) * 1024] = value.astype(BF)
+            s2_pass(h, j)
+    for h in (0, 1):
+        s2_final(h)
+    w_finish()
 
     def last(i, _):
         act_copy(i, c, (c + 16 - i) % 16).wait_recv()
-        w3_copy(i, r, (r + 16 - i) % 16).wait_recv()
         act_copy(i, (c + i) % 16, c).wait_send()
         cot_copy(i, (c + i) % 16, c).wait_send()
         w1_copy(i, (r + i) % 16, r).wait_send()
-        w2_copy(i, (c + i) % 16, c).wait_send()
         w3_copy(i, (r + i) % 16, r).wait_send()
         return 0
 
     lax.fori_loop(1, 16, last, 0)
+
+    def last_z(i, _):
+        w2_copy(i, (z + i) % 8, z).wait_send()
+        return 0
+
+    lax.fori_loop(1, 8, last_z, 0)
     for copy in sent:
         copy.wait_send()
 
@@ -458,14 +532,14 @@
         out_shape=(
             jax.ShapeDtypeStruct((32, 2048), BF),
             jax.ShapeDtypeStruct((32, 2048), BF),
-            jax.ShapeDtypeStruct((512, 512), BF),
+            jax.ShapeDtypeStruct((16, 2, 16, 512), BF),
         ),
         in_specs=[pl.BlockSpec(memory_space=pltpu.SMEM)] * 2 + [vspec] * 6,
         out_specs=(vspec,) * 3,
         scratch_shapes=[
             vm((2048, 2048), BF),
-            vm((8, 128, 128), BF),
-            vm((2, 4, 4, 32, 1024), BF),
+            vm((16, 128, 1024), BF),
+            vm((16, 4, 4, 32, 128), BF),
             vm((512, 128), BF),
             vm((8, 512, 128), F32),
             vm((8, 512, 128), F32),
@@ -476,18 +550,21 @@
             vm((512, 128), BF),
             vm((512, 128), BF),
             vm((512, 128), BF),
+            vm((512, 128), BF),
             vm((8, 2, 512, 128), BF),
             vm((512, 2048), F32),
             vm((2, 4, 3, 32, 1024), BF),
             vm((2, 4, 2, 16, 1024), BF),
             vm((2, 4, 2, 32, 1024), BF),
             vm((2, 4, 32, 1024), F32),
-            vm((2, 3, 32, 1024), F32),
-            vm((2, 2, 16, 1024), F32),
-            vm((2, 2, 32, 1024), F32),
-            vm((512, 512), BF),
-            vm((16, 32, 512), BF),
-            vm((16, 32, 512), BF),
+            vm((2, 3, 32, 1024), BF),
+            vm((2, 2, 16, 1024), BF),
+            vm((2, 2, 32, 1024), BF),
+            vm((16, 2, 16, 512), BF),
+            vm((16, 16, 512), BF),
+            vm((16, 16, 512), BF),
+            vm((16, 16, 512), BF),
+            vm((8, 16, 512), BF),
         ]
         + [dma((16,))] * 2
         + [dma((2, 5, 4))] * 2
@@ -497,7 +574,10 @@
         + [dma((2, 4, NS))] * 2
         + [dma((8,))] * 2
         + [dma((2, 5, 4))] * 2
-        + [dma((16,))] * 6,
+        + [dma((2,))] * 2
+        + [dma((16,))] * 2
+        + [dma((8,))] * 2
+        + [dma((16,))] * 2,
         compiler_params=pltpu.CompilerParams(
             collective_id=0, has_side_effects=True, vmem_limit_bytes=58 << 20
         ),
@@ -505,18 +585,22 @@
     )(cols, counts, src, dst, ew, xt, cot, weight)
 
 
-def finish_kernel(act_ref, fg_ref, wg_ref, act_out, fg_out, wg_out, wg_in, sems):
-    copies = [
-        pltpu.make_async_copy(wg_ref, wg_in, sems.at[0]),
-        pltpu.make_async_copy(act_ref, act_out, sems.at[1]),
-        pltpu.make_async_copy(fg_ref, fg_out, sems.at[2]),
+def finish_kernel(act_ref, fg_ref, wg_ref, act_out, fg_out, wg_out, act_in, fg_in, wg_in, sems):
+    pairs = ((wg_ref, wg_in), (act_ref, act_in), (fg_ref, fg_in))
+    copies = [pltpu.make_async_copy(src, dst, sems.at[i]) for i, (src, dst) in enumerate(pairs)]
+    copies += [
+        pltpu.make_async_copy(act_in, act_out, sems.at[3]),
+        pltpu.make_async_copy(fg_in, fg_out, sems.at[4]),
     ]
-    for copy in copies:
+    for copy in copies[:3]:
         copy.start()
+    for i in (1, 2):
+        copies[i].wait()
+        copies[i + 2].start()
     copies[0].wait()
     wg_out[...] = wg_in[...].astype(F32)
-    copies[1].wait()
-    copies[2].wait()
+    copies[3].wait()
+    copies[4].wait()
 
 
 def finish(act, fg, wg):
@@ -530,10 +614,15 @@
         ),
         in_specs=[anywhere] * 3,
         out_specs=(anywhere, anywhere, pl.BlockSpec(memory_space=pltpu.VMEM)),
-        scratch_shapes=[pltpu.VMEM((512, 512), BF), pltpu.SemaphoreType.DMA((3,))],
+        scratch_shapes=[
+            pltpu.VMEM((32, 2048), BF),
+            pltpu.VMEM((32, 2048), BF),
+            pltpu.VMEM((512, 512), BF),
+            pltpu.SemaphoreType.DMA((5,)),
+        ],
         compiler_params=pltpu.CompilerParams(vmem_limit_bytes=58 << 20),
         name="finish",
-    )(act, fg, wg)
+    )(act, fg, wg.reshape(512, 512))
 
 
 def shards(features, weight, block_cols, block_count, edge_src, edge_dst, edge_weight, cotangent):

time: 109 us -> 97.3 us (0.89)
  Pallas kernels: 108 us -> 96.3 us
    pallas_call x1, Pallas kernels: 10 us -> 2.77 us  [finish(): pl.pallas_call(finish_kernel, out_shape=(jax.ShapeDtypeStruct((32, 2048),...]
    pallas_call x1, Pallas kernels: 98.3 us -> 93.6 us  [layer(): pl.pallas_call(layer_kernel, out_shape=(jax.ShapeDtypeStruct((32, 2048),...]
where the time goes in v3:
time: 97.3 us; the launch traced here: 97.1 us
  Pallas kernels  96.3 us (99%)
    pallas_call x1, Pallas kernels, layer(): pl.pallas_call(layer_kernel, out_shape=(jax.ShapeDtypeStruct((32, 2048),...  93.6 us
    pallas_call x1, Pallas kernels, finish(): pl.pallas_call(finish_kernel, out_shape=(jax.ShapeDtypeStruct((32, 2048),...  2.77 us

profile of v3, /device:TPU:1, one launch (start us, length us, event | category | flops | bytes accessed | tf_op | source)
XLA Modules:
  0.0 97.1 jit_solution(8439091310246002351)
XLA Ops:
  0.6 93.6 %layer.1 = (bf16[32,2048]{1,0:T(8,128)(2,1)}, bf16[32,2048]{1,0:T(8,128)(2,1)}, bf16[16,2,16,512]{3,2,1,0:T(8,128)(2,1)}) custom-call(s32[8,16]{1,0:T(8,128)} %bitcast.18, s32[1,16]{1,0:T(1,128)} %bitcast.19, s32[16,8,512]{2,1,0:T(8,128)} %bitcast.13, s32[16,8,512]{2,1,0:T(8,128)} %bitcast.14, bf16[16,8,512]{2,1,0:T(8,128)(2,1)} %bitcast.15, ...), custom_call_target="tpu_custom_call" | custom-call | tf_op jit(solution)/shard_map/layer/pallas_call | solution.py:530
  94.2 2.8 %finish.1 = (bf16[32,2048]{1,0:T(8,128)(2,1)}, bf16[32,2048]{1,0:T(8,128)(2,1)}, f32[512,512]{1,0:T(8,128)}) custom-call(bf16[32,2048]{1,0:T(8,128)(2,1)} %get-tuple-element.9.act_ref, bf16[32,2048]{1,0:T(8,128)(2,1)} %get-tuple-element.10.fg_ref, bf16[512,512]{1,0:T(8,128)(2,1)} %bitcast.12), custom_call_target="tpu_custom_call" | custom-call | tf_op jit(solution)/shard_map/finish/pallas_call | solution.py:608

commit v4 on v3

--- a/solution.py
+++ b/solution.py
@@ -17,8 +17,8 @@
 def layer_kernel(
     cols_ref, counts_ref, src_ref, dst_ref, ew_ref, xt_ref, cot_ref, w_ref,
     act_ref, fg_ref, wg_ref,
-    a, tiles, xg, cotb, pown, psend, precv, zr, zs, axb, axl, actb, slb, sll, tg, acc,
-    xs1, xr1h, xr1f, s1, xs2, xr2h, xr2f,
+    a, tiles, xg0, xg1, xg2, xg3, wt, cotb, pown, psend, precv, zr, zs, axb, axl, actb, slb, sll, tg, acc,
+    xs1, xr1h, xr1f, s1, xs2, xr2,
     wp, w0r, w0s, w1r, wz,
     cot_ss, cot_rs, ag_ss, ag_rs, core_ss, core_rs, rz_ss, rz_rs,
     act_ss, act_rs, gz_ss, gz_rs, gc_ss, gc_rs, rx_ss, rx_rs,
@@ -45,6 +45,7 @@
             src_ref=src, dst_ref=dst, send_sem=ss, recv_sem=rs, device_id=dev, device_id_type=MESH
         )
 
+    xg = (xg0, xg1, xg2, xg3)
     sent = []
 
     def send(src, dst, ss, rs, dev):
@@ -63,10 +64,8 @@
         return 0
 
     lax.fori_loop(1, 16, greet, 0)
-    for h in (0, 1):
-        for b in range(h * 8, h * 8 + 8):
-            xg[b, x, y] = xt_ref[:, b * 128 : (b + 1) * 128]
-    pl.semaphore_wait(barrier, 30)
+    for b in range(16):
+        xg0[b, y] = xt_ref[:, b * 128 : (b + 1) * 128]
 
     spots = lax.broadcasted_iota(jnp.int32, (128, 512), 0).astype(F32).astype(BF)
     slots = lax.broadcasted_iota(jnp.int32, (8, 512), 0)
@@ -116,44 +115,66 @@
     def place(start, stop):
         over(place_block, start, stop)
 
+    eye = lax.broadcasted_iota(jnp.int32, (512, 512), 0) == lax.broadcasted_iota(jnp.int32, (512, 512), 1)
+    wt[...] = lax.dot_general(
+        jnp.where(eye, 1.0, 0.0).astype(BF), w_ref[...], NT, preferred_element_type=F32
+    ).astype(BF)
+    make(0, 5)
+    pl.semaphore_wait(barrier, 30)
+
     def xg_at(h, o1, o2):
-        if h == 0:
-            return xg.at[0:8, (x + o2) % 4, (y + o1) % 4]
-        return xg.at[8:16, (x + o1) % 4, (y + o2) % 4]
-
-    def axis(h, ring):
-        return (at_y, at_x)[(h + ring) % 2]
-
-    def ag_send(h, ring, lane, j, piece):
-        dev = axis(h, ring)(1 if j % 2 == 0 else -1)
-        if j == 2:
-            piece = piece.at[:, 0:16]
-        if j == 3:
-            piece = piece.at[:, 16:32]
-        send(piece, piece, ag_ss.at[h, lane, j], ag_rs.at[h, lane, j], dev)
-
-    def ag_got(h, ring, lane, j, piece):
-        dev = axis(h, ring)(-1 if j % 2 == 0 else 1)
-        if j == 2:
-            piece = piece.at[:, 0:16]
-        if j == 3:
-            piece = piece.at[:, 16:32]
+        ox, oy = ((o2, o1), (o1, o2))[h]
+        return xg[ox % 4].at[8 * h : 8 * h + 8, (y + oy) % 4]
+
+    def along_x(h, ring):
+        return (h + ring) % 2 == 1
+
+    def ag_send(h, ring, lane, j, o1, o2):
+        step = (1, -1, 1, -1)[j] if ring == 1 else (1, -1, 2)[j]
+        src = xg_at(h, o1, o2)
+        if along_x(h, ring):
+            dst = xg_at(h, o1 - step, o2) if ring == 0 else xg_at(h, o1, o2 - step)
+            dev = at_x(step)
+        else:
+            dst = src
+            dev = at_y(step)
+        if ring == 1 and j >= 2:
+            rows = slice(0, 16) if j == 2 else slice(16, 32)
+            src, dst = src.at[:, rows], dst.at[:, rows]
+        send(src, dst, ag_ss.at[h, lane, j], ag_rs.at[h, lane, j], dev)
+
+    def ag_got(h, ring, lane, j):
+        if ring == 0:
+            step = (1, -1, 2)[j]
+            piece = xg_at(h, -step, 0)
+        else:
+            step = (1, -1, 1, -1)[j]
+            piece = xg_at(h, lane - 1, -step if j < 2 else 2)
+            if j >= 2:
+                piece = piece.at[:, slice(0, 16) if j == 2 else slice(16, 32)]
+        dev = at_x(-step) if along_x(h, ring) else at_y(-step)
         got(piece, ag_ss.at[h, lane, j], ag_rs.at[h, lane, j], dev)
 
     def ag_ring2_own(h, o1):
         for j in (0, 1):
-            ag_send(h, 1, 1 + o1, j, xg_at(h, o1, 0))
+            ag_send(h, 1, 1 + o1, j, o1, 0)
 
     def ag_ring2_pass(h, o1):
         for j, o in ((0, 3), (1, 1)):
-            ag_got(h, 1, 1 + o1, j, xg_at(h, o1, o))
-            ag_send(h, 1, 1 + o1, 2 + j, xg_at(h, o1, o))
+            ag_got(h, 1, 1 + o1, j)
+            ag_send(h, 1, 1 + o1, 2 + j, o1, o)
+
+    def ag_ring2_end(h, o1):
+        for j in (2, 3):
+            ag_got(h, 1, 1 + o1, j)
 
     for h in (0, 1):
         for j in (0, 1):
-            ag_send(h, 0, 0, j, xg_at(h, 0, 0))
+            ag_send(h, 0, 0, j, 0, 0)
     for h in (0, 1):
         ag_ring2_own(h, 0)
+    for h in (0, 1):
+        ag_send(h, 0, 0, 2, 0, 0)
 
     def cot_copy(i, peer, mine):
         return rc(
@@ -169,104 +190,133 @@
     lax.fori_loop(1, 16, cot_send, 0)
     cotb[pl.ds(pl.multiple_of(c * 32, 32), 32), :] = cot_ref[:, pl.ds(pl.multiple_of(c * 128, 128), 128)]
 
-    make(0, 3)
+    make(5, 7)
     for j, o in ((0, 3), (1, 1)):
         for h in (0, 1):
-            ag_got(h, 0, 0, j, xg_at(h, o, 0))
-            ag_send(h, 0, 0, 2 + j, xg_at(h, o, 0))
+            ag_got(h, 0, 0, j)
             ag_ring2_own(h, o)
-    make(3, 6)
     for h in (0, 1):
+        ag_got(h, 0, 0, 2)
+        ag_ring2_own(h, 2)
+    for h in (1, 0):
         ag_ring2_pass(h, 0)
-    for h in (0, 1):
-        for j in (2, 3):
-            ag_got(h, 0, 0, j, xg_at(h, 2, 0))
-        ag_ring2_own(h, 2)
-    make(6, 9)
+    make(7, 10)
     for o1 in (3, 1):
         for h in (0, 1):
             ag_ring2_pass(h, o1)
-    make(9, 12)
+    ag_ring2_end(1, 0)
+
+    def block_product(offsets, g):
+        picked = []
+        for s in range(8):
+            col = cols_ref[s, g]
+            rows = [xg[o][col].reshape(128, 128) for o in offsets]
+            picked.append(rows[0] if len(rows) == 1 else jnp.concatenate(rows, axis=0))
+        left = jnp.concatenate(picked, axis=1)
+        return lax.dot_general(left, tiles[g], NT, preferred_element_type=F32)
+
+    def product(offsets, *ds):
+        for d in ds:
+            first = (z + d) % 8 * 2
+            value = block_product(offsets, first + 1 - k)
+            for i, o in enumerate(offsets):
+                psend[o, d] = value[128 * i : 128 * i + 128]
+                send(psend.at[o, d], precv.at[o, d], core_ss.at[o, d], core_rs.at[o, d], twin)
+            value = block_product(offsets, first + k)
+            for i, o in enumerate(offsets):
+                pown[o, d] = value[128 * i : 128 * i + 128]
+
+    def twin_got(o, d):
+        got(precv.at[o, d], core_ss.at[o, d], core_rs.at[o, d], twin)
+
+    HALVES = (slice(0, 64), slice(64, 128))
+
+    def z_step(offsets, dist):
+        for o in offsets:
+            for d in (4,) if dist == 4 else (dist, 8 - dist):
+                twin_got(o, d)
+            for side in (0, 1):
+                d = dist if side == 0 else 8 - dist
+                sems = (rz_ss.at[side, dist, o], rz_rs.at[side, dist, o])
+                before = (rz_ss.at[side, dist + 1, o], rz_rs.at[side, dist + 1, o]) if dist < 4 else None
+                came, goes = at_z(-1 if side == 0 else 1), at_z(1 if side == 0 else -1)
+                if dist == 4:
+                    half = HALVES[side]
+                    zs[side, 4, o, half] = (pown[o, d, half] + precv[o, d, half]).astype(BF)
+                    send(zs.at[side, 4, o, half], zr.at[side, 3, o, half], *sems, goes)
+                    continue
+                value = pown[o, d] + precv[o, d]
+                if dist == 3:
+                    half, other = HALVES[side], HALVES[1 - side]
+                    got(zr.at[side, 3, o, half], *before, came)
+                    zs[side, 3, o, half] = (value[half] + zr[side, 3, o, half].astype(F32)).astype(BF)
+                    zs[side, 3, o, other] = value[other].astype(BF)
+                else:
+                    got(zr.at[side, dist, o], *before, came)
+                    zs[side, dist, o] = (value + zr[side, dist, o].astype(F32)).astype(BF)
+                send(zs.at[side, dist, o], zr.at[side, dist - 1, o], *sems, goes)
+
+    def z_last(offsets):
+        for o in offsets:
+            twin_got(o, 0)
+            value = pown[o, 0] + precv[o, 0]
+            for side in (0, 1):
+                got(zr.at[side, 0, o], rz_ss.at[side, 1, o], rz_rs.at[side, 1, o], at_z(-1 if side == 0 else 1))
+                value = value + zr[side, 0, o].astype(F32)
+            rows = pl.ds(pl.multiple_of((x + o) % 4 * 128, 128), 128)
+            high = value.astype(BF)
+            axb[rows] = high
+            axl[rows] = (value - high.astype(F32)).astype(BF)
+
+    G0, G1, G2 = (0,), (1, 3), (2,)
+    product(G0, 4)
     for h in (0, 1):
         ag_ring2_pass(h, 2)
-    make(12, 16)
+    make(10, 16)
+    product(G0, 3, 5)
+    z_step(G0, 4)
+    product(G0, 2, 6)
+    for o1 in (3, 1):
+        ag_ring2_end(1, o1)
+    product(G1, 4)
+    z_step(G0, 3)
+    product(G1, 3, 5)
+    z_step(G1, 4)
     for o1 in (0, 3, 1, 2):
-        for h in (0, 1):
-            for j in (2, 3):
-                ag_got(h, 1, 1 + o1, j, xg_at(h, o1, 2))
-
-    def block_product(g):
-        picked = []
-        for s in range(8):
-            picked.append(xg[cols_ref[s, g]].reshape(512, 128))
-        left = jnp.concatenate(picked, axis=1)
-        return lax.dot_general(left, tiles[g], NT, preferred_element_type=F32)
-
-    def product(d):
-        first = (z + d) % 8 * 2
-        psend[d] = block_product(first + 1 - k)
-        send(psend.at[d], precv.at[d], core_ss.at[d], core_rs.at[d], twin)
-        pown[d] = block_product(first + k)
-
-    def twin_got(d):
-        got(precv.at[d], core_ss.at[d], core_rs.at[d], twin)
-
-    def z_rows(side, dist, j):
-        return dist < 4 or (j < NS // 2) == (side == 0)
-
-    def z_step(dist):
-        offsets = (4,) if dist == 4 else (dist, 8 - dist)
-        for d in offsets:
-            twin_got(d)
-        for j in range(NS):
-            rows = pl.ds(j * SUB, SUB)
-            for side in (0, 1):
-                if not z_rows(side, dist, j):
-                    continue
-                d = dist if side == 0 else (8 - dist) % 8
-                value = pown[d, rows] + precv[d, rows]
-                if dist < 4 and z_rows(side, dist + 1, j):
-                    got(zr.at[side, dist, rows], rz_ss.at[side, dist + 1, j], rz_rs.at[side, dist + 1, j], at_z(-1 if side == 0 else 1))
-                    value = value + zr[side, dist, rows].astype(F32)
-                zs[side, dist, rows] = value.astype(BF)
-                send(
-                    zs.at[side, dist, rows], zr.at[side, dist - 1, rows],
-                    rz_ss.at[side, dist, j], rz_rs.at[side, dist, j], at_z(1 if side == 0 else -1),
-                )
-
-    product(4)
-    product(3)
-    product(5)
-    z_step(4)
-    product(2)
-    product(6)
-    place(0, 2)
-    z_step(3)
-    product(1)
-    product(7)
-    place(2, 5)
-    z_step(2)
-    product(0)
-    place(5, 10)
-    z_step(1)
+        ag_ring2_end(0, o1)
+    ag_ring2_end(1, 2)
+    product(G2, 4)
+    product(G0, 1, 7)
+    z_step(G0, 2)
+    product(G1, 2, 6)
+    z_step(G1, 3)
+    product(G2, 3, 5)
+    z_step(G2, 4)
+    product(G0, 0)
+    z_step(G0, 1)
+    product(G1, 1, 7)
+    z_step(G1, 2)
+    product(G2, 2, 6)
+    z_step(G2, 3)
+    product(G1, 0)
+    z_step(G1, 1)
+    product(G2, 1, 7)
+    z_step(G2, 2)
+    product(G2, 0)
+    place(0, 4)
+    z_step(G2, 1)
+    place(4, 10)
+    z_last(G0 + G1)
     place(10, 16)
-    twin_got(0)
-    for j in range(NS):
-        rows = pl.ds(j * SUB, SUB)
-        value = pown[0, rows] + precv[0, rows]
-        for side in (0, 1):
-            got(zr.at[side, 0, rows], rz_ss.at[side, 1, j], rz_rs.at[side, 1, j], at_z(-1 if side == 0 else 1))
-            value = value + zr[side, 0, rows].astype(F32)
-        axb[rows] = value.astype(BF)
-        axl[rows] = (value - axb[rows].astype(F32)).astype(BF)
+    z_last(G2)
 
     def cot_wait(i, _):
         cot_copy(i, c, (c + 16 - i) % 16).wait_recv()
         return 0
 
     lax.fori_loop(1, 16, cot_wait, 0)
-    hidden = lax.dot_general(w_ref[...], axb[...], TN, preferred_element_type=F32)
-    hidden = hidden + lax.dot_general(w_ref[...], axl[...], TN, preferred_element_type=F32)
+    hidden = jnp.dot(wt[...], axb[...], preferred_element_type=F32)
+    hidden = hidden + jnp.dot(wt[...], axl[...], preferred_element_type=F32)
     sig = jax.nn.sigmoid(hidden)
     actb[...] = (hidden * sig).astype(BF)
     slope = cotb[...].astype(F32) * sig * (1.0 + hidden * (1.0 - sig))
@@ -377,6 +427,9 @@
         lax.fori_loop(1, 16, w3_wait, 0)
         send(wg_ref.at[:, k], wg_ref.at[:, k], w0_ss.at[1], w0_rs.at[1], twin)
         got(wg_ref.at[:, 1 - k], w0_ss.at[1], w0_rs.at[1], twin)
+
+    def z_rows(side, dist, j):
+        return dist < 4 or (j < NS // 2) == (side == 0)
 
     def gather_step(dist):
         for j in range(NS):
@@ -405,9 +458,8 @@
             gc_got(d)
             acc[...] += back_part(d)
         gather_step(dist + 2)
-    lax.fori_loop(1, 16, act_send, 0)
-    act_ref[:, pl.ds(pl.multiple_of(c * 128, 128), 128)] = actb[pl.ds(pl.multiple_of(c * 32, 32), 32), :]
-    w_start_z()
+        if dist == 1:
+            w_start_z()
     for d in (3, 5):
         gc_got(d)
         acc[...] += back_part(d)
@@ -462,22 +514,15 @@
             rx(None, xr1f.at[h, o2, j], h, 0, o2, 2 + j, False)
         s1[h, o2] = q(h, 0, o2, None) + xr1f[h, o2, 0].astype(F32) + xr1f[h, o2, 1].astype(F32)
 
-    def s2_halves(h):
-        for j in (0, 1):
-            xs2[h, 0, 16 * j : 16 * j + 16] = s1[h, 2, 16 * j : 16 * j + 16].astype(BF)
-            rx(xs2.at[h, 0, 16 * j : 16 * j + 16], xr2h.at[h, j], h, 1, 4, j, True)
-
-    def s2_pass(h, j):
-        o = (1, 3)[j]
-        rx(None, xr2h.at[h, j], h, 1, 4, j, False)
-        xs2[h, 1 + j, 16 * j : 16 * j + 16] = (s1[h, o, 16 * j : 16 * j + 16] + xr2h[h, j].astype(F32)).astype(BF)
-        xs2[h, 1 + j, 16 - 16 * j : 32 - 16 * j] = s1[h, o, 16 - 16 * j : 32 - 16 * j].astype(BF)
-        rx(xs2.at[h, 1 + j], xr2f.at[h, j], h, 1, 4, 2 + j, True)
+    def s2_send(h, o2):
+        xs2[h, o2 - 1] = s1[h, o2].astype(BF)
+        send(xs2.at[h, o2 - 1], xr2.at[h, o2 - 1], rx_ss.at[h, 4, o2], rx_rs.at[h, 4, o2], rx_axis(h, 1)(o2))
 
     def s2_final(h):
-        for j in (0, 1):
-            rx(None, xr2f.at[h, j], h, 1, 4, 2 + j, False)
-        value = s1[h, 0] + xr2f[h, 0].astype(F32) + xr2f[h, 1].astype(F32)
+        value = s1[h, 0]
+        for o2 in (2, 1, 3):
+            got(xr2.at[h, o2 - 1], rx_ss.at[h, 4, o2], rx_rs.at[h, 4, o2], rx_axis(h, 1)(-o2))
+            value = value + xr2[h, o2 - 1].astype(F32)
         fg_ref[:, h * 1024 : (h + 1) * 1024] = value.astype(BF)
 
     last_part(2)
@@ -487,6 +532,8 @@
     for o in (1, 3, 0):
         last_part(o)
         s1_halves(1, o)
+    lax.fori_loop(1, 16, act_send, 0)
+    act_ref[:, pl.ds(pl.multiple_of(c * 128, 128), 128)] = actb[pl.ds(pl.multiple_of(c * 32, 32), 32), :]
     for o2 in ORDER:
         for h in (0, 1):
             for j in (0, 1):
@@ -495,11 +542,8 @@
     for o2 in ORDER:
         for h in (0, 1):
             s1_final(h, o2)
-            if o2 == 2:
-                s2_halves(h)
-    for h in (0, 1):
-        for j in (0, 1):
-            s2_pass(h, j)
+            if o2 > 0:
+                s2_send(h, o2)
     for h in (0, 1):
         s2_final(h)
     w_finish()
@@ -539,13 +583,17 @@
         scratch_shapes=[
             vm((2048, 2048), BF),
             vm((16, 128, 1024), BF),
-            vm((16, 4, 4, 32, 128), BF),
+            vm((16, 4, 32, 128), BF),
+            vm((16, 4, 32, 128), BF),
+            vm((16, 4, 32, 128), BF),
+            vm((16, 4, 32, 128), BF),
+            vm((512, 512), BF),
             vm((512, 128), BF),
-            vm((8, 512, 128), F32),
-            vm((8, 512, 128), F32),
-            vm((8, 512, 128), F32),
-            vm((2, 4, 512, 128), BF),
-            vm((2, 5, 512, 128), BF),
+            vm((4, 8, 128, 128), F32),
+            vm((4, 8, 128, 128), F32),
+            vm((4, 8, 128, 128), F32),
+            vm((2, 4, 4, 128, 128), BF),
+            vm((2, 5, 4, 128, 128), BF),
             vm((512, 128), BF),
             vm((512, 128), BF),
             vm((512, 128), BF),
@@ -558,8 +606,7 @@
             vm((2, 4, 2, 32, 1024), BF),
             vm((2, 4, 32, 1024), F32),
             vm((2, 3, 32, 1024), BF),
-            vm((2, 2, 16, 1024), BF),
-            vm((2, 2, 32, 1024), BF),
+            vm((2, 3, 32, 1024), BF),
             vm((16, 2, 16, 512), BF),
             vm((16, 16, 512), BF),
             vm((16, 16, 512), BF),
@@ -568,8 +615,8 @@
         ]
         + [dma((16,))] * 2
         + [dma((2, 5, 4))] * 2
-        + [dma((8,))] * 2
-        + [dma((2, 5, NS))] * 2
+        + [dma((4, 8))] * 2
+        + [dma((2, 5, 4))] * 2
         + [dma((16,))] * 2
         + [dma((2, 4, NS))] * 2
         + [dma((8,))] * 2

time: 97.3 us -> 101 us (1.038)
  Pallas kernels: 96.3 us -> 100 us
    pallas_call x1, Pallas kernels: 93.6 us -> 97.3 us  [layer(): pl.pallas_call(layer_kernel, out_shape=(jax.ShapeDtypeStruct((32, 2048),...]
where the time goes in v4:
time: 101 us
  Pallas kernels  100 us (99%)
    pallas_call x1, Pallas kernels, layer(): pl.pallas_call(layer_kernel, out_shape=(jax.ShapeDtypeStruct((32, 2048),...  97.3 us
    pallas_call x1, Pallas kernels, finish(): pl.pallas_call(finish_kernel, out_shape=(jax.ShapeDtypeStruct((32, 2048),...  2.77 us

profile of v4, /device:TPU:1, one launch (start us, length us, event | category | flops | bytes accessed | tf_op | source)
XLA Modules:
  0.0 100.9 jit_solution(3876087959098885317)
XLA Ops:
  0.6 97.3 %layer.1 = (bf16[32,2048]{1,0:T(8,128)(2,1)}, bf16[32,2048]{1,0:T(8,128)(2,1)}, bf16[16,2,16,512]{3,2,1,0:T(8,128)(2,1)}) custom-call(s32[8,16]{1,0:T(8,128)} %bitcast.18, s32[1,16]{1,0:T(1,128)} %bitcast.19, s32[16,8,512]{2,1,0:T(8,128)} %bitcast.13, s32[16,8,512]{2,1,0:T(8,128)} %bitcast.14, bf16[16,8,512]{2,1,0:T(8,128)(2,1)} %bitcast.15, ...), custom_call_target="tpu_custom_call" | custom-call | tf_op jit(solution)/shard_map/layer/pallas_call | solution.py:574
  97.9 2.8 %finish.1 = (bf16[32,2048]{1,0:T(8,128)(2,1)}, bf16[32,2048]{1,0:T(8,128)(2,1)}, f32[512,512]{1,0:T(8,128)}) custom-call(bf16[32,2048]{1,0:T(8,128)(2,1)} %get-tuple-element.9.act_ref, bf16[32,2048]{1,0:T(8,128)(2,1)} %get-tuple-element.10.fg_ref, bf16[512,512]{1,0:T(8,128)(2,1)} %bitcast.12), custom_call_target="tpu_custom_call" | custom-call | tf_op jit(solution)/shard_map/finish/pallas_call | solution.py:655

commit v5 on v4

--- a/solution.py
+++ b/solution.py
@@ -9,17 +9,18 @@
 BF = jnp.bfloat16
 F32 = jnp.float32
 NT = (((1,), (1,)), ((), ()))
-TN = (((0,), (0,)), ((), ()))
 NS = 4
 SUB = 512 // NS
 
 
 def layer_kernel(
-    cols_ref, counts_ref, src_ref, dst_ref, ew_ref, xt_ref, cot_ref, w_ref,
-    act_ref, fg_ref, wg_ref,
+    cols_in, counts_in, src_in, dst_in, ew_in, xt_in, cot_in, w_in,
+    act_out, fg_out, wg_out,
+    cols_ref, counts_ref, src_ref, dst_ref, ew_ref, xt_ref, cot_ref, w_ref, act_ref, fg_ref, wg_ref,
     a, tiles, xg0, xg1, xg2, xg3, wt, cotb, pown, psend, precv, zr, zs, axb, axl, actb, slb, sll, tg, acc,
     xs1, xr1h, xr1f, s1, xs2, xr2,
     wp, w0r, w0s, w1r, wz,
+    in_sem, out_sem,
     cot_ss, cot_rs, ag_ss, ag_rs, core_ss, core_rs, rz_ss, rz_rs,
     act_ss, act_rs, gz_ss, gz_rs, gc_ss, gc_rs, rx_ss, rx_rs,
     w0_ss, w0_rs, w1_ss, w1_rs, w2_ss, w2_rs, w3_ss, w3_rs,
@@ -56,6 +57,14 @@
     def got(ref, ss, rs, dev):
         rc(ref, ref, ss, rs, dev).wait_recv()
 
+    pairs = (
+        (xt_in, xt_ref), (w_in, w_ref), (cols_in, cols_ref), (counts_in, counts_ref),
+        (src_in, src_ref), (dst_in, dst_ref), (ew_in, ew_ref), (cot_in, cot_ref),
+    )
+    loads = [pltpu.make_async_copy(src, dst, in_sem.at[i]) for i, (src, dst) in enumerate(pairs)]
+    for load in loads:
+        load.start()
+
     barrier = pltpu.get_barrier_semaphore()
 
     def greet(i, _):
@@ -64,6 +73,7 @@
         return 0
 
     lax.fori_loop(1, 16, greet, 0)
+    loads[0].wait()
     for b in range(16):
         xg0[b, y] = xt_ref[:, b * 128 : (b + 1) * 128]
 
@@ -115,11 +125,14 @@
     def place(start, stop):
         over(place_block, start, stop)
 
+    loads[1].wait()
     eye = lax.broadcasted_iota(jnp.int32, (512, 512), 0) == lax.broadcasted_iota(jnp.int32, (512, 512), 1)
     wt[...] = lax.dot_general(
         jnp.where(eye, 1.0, 0.0).astype(BF), w_ref[...], NT, preferred_element_type=F32
     ).astype(BF)
-    make(0, 5)
+    for load in loads[2:]:
+        load.wait()
+    make(0, 4)
     pl.semaphore_wait(barrier, 30)
 
     def xg_at(h, o1, o2):
@@ -190,16 +203,16 @@
     lax.fori_loop(1, 16, cot_send, 0)
     cotb[pl.ds(pl.multiple_of(c * 32, 32), 32), :] = cot_ref[:, pl.ds(pl.multiple_of(c * 128, 128), 128)]
 
-    make(5, 7)
+    make(4, 7)
     for j, o in ((0, 3), (1, 1)):
         for h in (0, 1):
             ag_got(h, 0, 0, j)
             ag_ring2_own(h, o)
+    for h in (1, 0):
+        ag_ring2_pass(h, 0)
     for h in (0, 1):
         ag_got(h, 0, 0, 2)
         ag_ring2_own(h, 2)
-    for h in (1, 0):
-        ag_ring2_pass(h, 0)
     make(7, 10)
     for o1 in (3, 1):
         for h in (0, 1):
@@ -269,45 +282,44 @@
             axl[rows] = (value - high.astype(F32)).astype(BF)
 
     G0, G1, G2 = (0,), (1, 3), (2,)
-    product(G0, 4)
+    product(G0, 4, 3, 5)
+    z_step(G0, 4)
     for h in (0, 1):
         ag_ring2_pass(h, 2)
-    make(10, 16)
-    product(G0, 3, 5)
-    z_step(G0, 4)
-    product(G0, 2, 6)
+    make(10, 13)
     for o1 in (3, 1):
         ag_ring2_end(1, o1)
     product(G1, 4)
     z_step(G0, 3)
     product(G1, 3, 5)
     z_step(G1, 4)
+    make(13, 16)
     for o1 in (0, 3, 1, 2):
         ag_ring2_end(0, o1)
     ag_ring2_end(1, 2)
     product(G2, 4)
-    product(G0, 1, 7)
+    product(G0, 2, 6)
+    z_step(G2, 4)
     z_step(G0, 2)
     product(G1, 2, 6)
     z_step(G1, 3)
     product(G2, 3, 5)
-    z_step(G2, 4)
-    product(G0, 0)
+    z_step(G2, 3)
+    product(G0, 1, 7)
     z_step(G0, 1)
     product(G1, 1, 7)
     z_step(G1, 2)
     product(G2, 2, 6)
-    z_step(G2, 3)
+    z_step(G2, 2)
     product(G1, 0)
     z_step(G1, 1)
     product(G2, 1, 7)
-    z_step(G2, 2)
+    z_step(G2, 1)
+    product(G0, 0)
     product(G2, 0)
-    place(0, 4)
-    z_step(G2, 1)
-    place(4, 10)
+    place(14, 16)
     z_last(G0 + G1)
-    place(10, 16)
+    place(10, 14)
     z_last(G2)
 
     def cot_wait(i, _):
@@ -322,19 +334,19 @@
     slope = cotb[...].astype(F32) * sig * (1.0 + hidden * (1.0 - sig))
     slb[...] = slope.astype(BF)
     sll[...] = (slope - slb[...].astype(F32)).astype(BF)
-    tg[z, k] = (
-        jnp.dot(w_ref[...], slb[...], preferred_element_type=F32)
-        + jnp.dot(w_ref[...], sll[...], preferred_element_type=F32)
-    ).astype(BF)
+    ORDER = (2, 1, 3, 0)
+
+    def gz_piece(side, dist, j):
+        owner = (z - dist + 8) % 8 if side == 0 else (z + dist) % 8
+        feats = pl.ds(pl.multiple_of((x + ORDER[j]) % 4 * 128, 128), 128)
+        return tg.at[owner, k, feats]
 
     def gz_send(side, dist, j):
-        owner = (z - dist + 8) % 8 if side == 0 else (z + dist) % 8
-        piece = tg.at[owner, k, pl.ds(j * SUB, SUB)]
+        piece = gz_piece(side, dist, j)
         send(piece, piece, gz_ss.at[side, dist, j], gz_rs.at[side, dist, j], at_z(1 if side == 0 else -1))
 
     def gz_got(side, dist, j):
-        owner = (z - dist + 8) % 8 if side == 0 else (z + dist) % 8
-        piece = tg.at[owner, k, pl.ds(j * SUB, SUB)]
+        piece = gz_piece(side, dist, j)
         got(piece, gz_ss.at[side, dist - 1, j], gz_rs.at[side, dist - 1, j], at_z(-1 if side == 0 else 1))
 
     def gc_send(d):
@@ -346,6 +358,11 @@
         got(piece, gc_ss.at[d], gc_rs.at[d], twin)
 
     for j in range(NS):
+        feats = pl.ds(pl.multiple_of((x + ORDER[j]) % 4 * 128, 128), 128)
+        tg[z, k, feats] = (
+            jnp.dot(w_ref[feats], slb[...], preferred_element_type=F32)
+            + jnp.dot(w_ref[feats], sll[...], preferred_element_type=F32)
+        ).astype(BF)
         for side in (0, 1):
             gz_send(side, 0, j)
     gc_send(0)
@@ -452,17 +469,22 @@
     acc[...] = back_part(0)
     gather_step(1)
     w_start_row()
+    place(6, 10)
     gather_step(2)
-    for dist in (1, 2):
-        for d in (dist, 8 - dist):
-            gc_got(d)
-            acc[...] += back_part(d)
-        gather_step(dist + 2)
-        if dist == 1:
-            w_start_z()
+    for d in (1, 7):
+        gc_got(d)
+        acc[...] += back_part(d)
+    place(2, 6)
+    gather_step(3)
+    w_start_z()
+    for d in (2, 6):
+        gc_got(d)
+        acc[...] += back_part(d)
+    place(0, 2)
     for d in (3, 5):
         gc_got(d)
         acc[...] += back_part(d)
+    gather_step(4)
     gc_got(4)
 
     def last_part(o):
@@ -494,8 +516,6 @@
             send(src, dst, rx_ss.at[h, lane, j], rx_rs.at[h, lane, j], dev)
         else:
             got(dst, rx_ss.at[h, lane, j], rx_rs.at[h, lane, j], dev)
-
-    ORDER = (2, 1, 3, 0)
 
     def s1_halves(h, o2):
         for j in (0, 1):
@@ -538,18 +558,30 @@
         for h in (0, 1):
             for j in (0, 1):
                 s1_pass(h, o2, j)
-    w_start_last()
+        if o2 == 1:
+            w_start_last()
     for o2 in ORDER:
         for h in (0, 1):
             s1_final(h, o2)
             if o2 > 0:
                 s2_send(h, o2)
+    w_finish()
+    wg_copy = pltpu.make_async_copy(wg_ref, wg_out, out_sem.at[0])
+    wg_copy.start()
+
+    def act_wait(i, _):
+        act_copy(i, c, (c + 16 - i) % 16).wait_recv()
+        return 0
+
+    lax.fori_loop(1, 16, act_wait, 0)
+    act_store = pltpu.make_async_copy(act_ref, act_out, out_sem.at[1])
+    act_store.start()
     for h in (0, 1):
         s2_final(h)
-    w_finish()
+    fg_store = pltpu.make_async_copy(fg_ref, fg_out, out_sem.at[2])
+    fg_store.start()
 
     def last(i, _):
-        act_copy(i, c, (c + 16 - i) % 16).wait_recv()
         act_copy(i, (c + i) % 16, c).wait_send()
         cot_copy(i, (c + i) % 16, c).wait_send()
         w1_copy(i, (r + i) % 16, r).wait_send()
@@ -565,12 +597,14 @@
     lax.fori_loop(1, 8, last_z, 0)
     for copy in sent:
         copy.wait_send()
+    for store in (wg_copy, act_store, fg_store):
+        store.wait()
 
 
 def layer(cols, counts, src, dst, ew, xt, cot, weight):
     dma = pltpu.SemaphoreType.DMA
     vm = pltpu.VMEM
-    vspec = pl.BlockSpec(memory_space=pltpu.VMEM)
+    anywhere = pl.BlockSpec(memory_space=pl.ANY)
     return pl.pallas_call(
         layer_kernel,
         out_shape=(
@@ -578,9 +612,20 @@
             jax.ShapeDtypeStruct((32, 2048), BF),
             jax.ShapeDtypeStruct((16, 2, 16, 512), BF),
         ),
-        in_specs=[pl.BlockSpec(memory_space=pltpu.SMEM)] * 2 + [vspec] * 6,
-        out_specs=(vspec,) * 3,
+        in_specs=[anywhere] * 8,
+        out_specs=(anywhere,) * 3,
         scratch_shapes=[
+            pltpu.SMEM((8, 16), jnp.int32),
+            pltpu.SMEM((1, 16), jnp.int32),
+            vm((16, 8, 512), jnp.int32),
+            vm((16, 8, 512), jnp.int32),
+            vm((16, 8, 512), BF),
+            vm((32, 2048), BF),
+            vm((32, 2048), BF),
+            vm((512, 512), BF),
+            vm((32, 2048), BF),
+            vm((32, 2048), BF),
+            vm((16, 2, 16, 512), BF),
             vm((2048, 2048), BF),
             vm((16, 128, 1024), BF),
             vm((16, 4, 32, 128), BF),
@@ -612,6 +657,8 @@
             vm((16, 16, 512), BF),
             vm((16, 16, 512), BF),
             vm((8, 16, 512), BF),
+            dma((8,)),
+            dma((3,)),
         ]
         + [dma((16,))] * 2
         + [dma((2, 5, 4))] * 2

time: 101 us -> 92.9 us (0.920)
  Pallas kernels: 100 us -> 92 us
    pallas_call x1, Pallas kernels: 97.3 us -> 89.2 us  [layer(): pl.pallas_call(layer_kernel, out_shape=(jax.ShapeDtypeStruct((32, 2048),...]
where the time goes in v5:
time: 92.9 us; the launch traced here: 92.8 us
  Pallas kernels  92 us (99%)
    pallas_call x1, Pallas kernels, layer(): pl.pallas_call(layer_kernel, out_shape=(jax.ShapeDtypeStruct((32, 2048),...  89.2 us
    pallas_call x1, Pallas kernels, finish(): pl.pallas_call(finish_kernel, out_shape=(jax.ShapeDtypeStruct((32, 2048),...  2.77 us

profile of v5, /device:TPU:1, one launch (start us, length us, event | category | flops | bytes accessed | tf_op | source)
XLA Modules:
  0.0 92.8 jit_solution(16850471169139038931)
XLA Ops:
  0.6 89.2 %layer.1 = (bf16[32,2048]{1,0:T(8,128)(2,1)}, bf16[32,2048]{1,0:T(8,128)(2,1)}, bf16[16,2,16,512]{3,2,1,0:T(8,128)(2,1)}) custom-call(s32[8,16]{1,0:T(8,128)} %bitcast.18, s32[1,16]{1,0:T(1,128)} %bitcast.19, s32[16,8,512]{2,1,0:T(8,128)} %bitcast.13, s32[16,8,512]{2,1,0:T(8,128)} %bitcast.14, bf16[16,8,512]{2,1,0:T(8,128)(2,1)} %bitcast.15, ...), custom_call_target="tpu_custom_call" | custom-call | tf_op jit(solution)/shard_map/layer/pallas_call | solution.py:608
  89.9 2.8 %finish.1 = (bf16[32,2048]{1,0:T(8,128)(2,1)}, bf16[32,2048]{1,0:T(8,128)(2,1)}, f32[512,512]{1,0:T(8,128)}) custom-call(bf16[32,2048]{1,0:T(8,128)(2,1)} %get-tuple-element.9.act_ref, bf16[32,2048]{1,0:T(8,128)(2,1)} %get-tuple-element.10.fg_ref, bf16[512,512]{1,0:T(8,128)(2,1)} %bitcast.12), custom_call_target="tpu_custom_call" | custom-call | tf_op jit(solution)/shard_map/finish/pallas_call | solution.py:702

commit v6 on v5

--- a/solution.py
+++ b/solution.py
@@ -9,20 +9,18 @@
 BF = jnp.bfloat16
 F32 = jnp.float32
 NT = (((1,), (1,)), ((), ()))
-NS = 4
-SUB = 512 // NS
 
 
 def layer_kernel(
     cols_in, counts_in, src_in, dst_in, ew_in, xt_in, cot_in, w_in,
     act_out, fg_out, wg_out,
     cols_ref, counts_ref, src_ref, dst_ref, ew_ref, xt_ref, cot_ref, w_ref, act_ref, fg_ref, wg_ref,
-    a, tiles, xg0, xg1, xg2, xg3, wt, cotb, pown, psend, precv, zr, zs, axb, axl, actb, slb, sll, tg, acc,
+    a, tiles, xg0, xg1, xg2, xg3, wt, cotb, pown, psend, precv, zr, zs, zfr, zfs, hid, axb, actb, slb, sll, tg, acc,
     xs1, xr1h, xr1f, s1, xs2, xr2,
     wp, w0r, w0s, w1r, wz,
     in_sem, out_sem,
-    cot_ss, cot_rs, ag_ss, ag_rs, core_ss, core_rs, rz_ss, rz_rs,
-    act_ss, act_rs, gz_ss, gz_rs, gc_ss, gc_rs, rx_ss, rx_rs,
+    cot_ss, cot_rs, ag_ss, ag_rs, core_ss, core_rs, rz_ss, rz_rs, zf_ss, zf_rs,
+    act_ss, act_rs, gz_ss, gz_rs, gf_ss, gf_rs, gc_ss, gc_rs, rx_ss, rx_rs,
     w0_ss, w0_rs, w1_ss, w1_rs, w2_ss, w2_rs, w3_ss, w3_rs,
 ):
     r = lax.axis_index("row")
@@ -67,12 +65,9 @@
 
     barrier = pltpu.get_barrier_semaphore()
 
-    def greet(i, _):
+    for i in (8, 7, 9, 6, 10, 5, 11, 4, 12, 3, 13, 2, 14, 1, 15):
+        pl.semaphore_signal(barrier, inc=1, device_id=(r, (c + i) % 16), device_id_type=MESH)
         pl.semaphore_signal(barrier, inc=1, device_id=((r + i) % 16, c), device_id_type=MESH)
-        pl.semaphore_signal(barrier, inc=1, device_id=(r, (c + i) % 16), device_id_type=MESH)
-        return 0
-
-    lax.fori_loop(1, 16, greet, 0)
     loads[0].wait()
     for b in range(16):
         xg0[b, y] = xt_ref[:, b * 128 : (b + 1) * 128]
@@ -252,6 +247,7 @@
                 d = dist if side == 0 else 8 - dist
                 sems = (rz_ss.at[side, dist, o], rz_rs.at[side, dist, o])
                 before = (rz_ss.at[side, dist + 1, o], rz_rs.at[side, dist + 1, o]) if dist < 4 else None
+                first = dist == 2 and o == 2
                 came, goes = at_z(-1 if side == 0 else 1), at_z(1 if side == 0 else -1)
                 if dist == 4:
                     half = HALVES[side]
@@ -264,22 +260,43 @@
                     got(zr.at[side, 3, o, half], *before, came)
                     zs[side, 3, o, half] = (value[half] + zr[side, 3, o, half].astype(F32)).astype(BF)
                     zs[side, 3, o, other] = value[other].astype(BF)
+                elif first:
+                    zs[side, dist, o] = value.astype(BF)
                 else:
                     got(zr.at[side, dist, o], *before, came)
                     zs[side, dist, o] = (value + zr[side, dist, o].astype(F32)).astype(BF)
                 send(zs.at[side, dist, o], zr.at[side, dist - 1, o], *sems, goes)
 
+    FAR = (4, 3, 5)
+
+    def z_far():
+        for i, d in enumerate(FAR):
+            twin_got(2, d)
+            zfs[i] = (pown[2, d] + precv[2, d]).astype(BF)
+            send(zfs.at[i], zfr.at[i], zf_ss.at[i], zf_rs.at[i], at_z(d))
+
     def z_last(offsets):
         for o in offsets:
             twin_got(o, 0)
             value = pown[o, 0] + precv[o, 0]
+            if o == 2:
+                for i, d in enumerate(FAR):
+                    got(zfr.at[i], zf_ss.at[i], zf_rs.at[i], at_z(-d))
+                    value = value + zfr[i].astype(F32)
             for side in (0, 1):
                 got(zr.at[side, 0, o], rz_ss.at[side, 1, o], rz_rs.at[side, 1, o], at_z(-1 if side == 0 else 1))
                 value = value + zr[side, 0, o].astype(F32)
-            rows = pl.ds(pl.multiple_of((x + o) % 4 * 128, 128), 128)
+            start = pl.multiple_of((x + o) % 4 * 128, 128)
             high = value.astype(BF)
-            axb[rows] = high
-            axl[rows] = (value - high.astype(F32)).astype(BF)
+            low = (value - high.astype(F32)).astype(BF)
+            axb[pl.ds(start, 128)] = high
+            weights = wt[:, pl.ds(start, 128)]
+            part = jnp.dot(
+                jnp.concatenate([weights, weights], axis=1),
+                jnp.concatenate([high, low], axis=0),
+                preferred_element_type=F32,
+            )
+            hid[...] = part if o == 0 else hid[...] + part
 
     G0, G1, G2 = (0,), (1, 3), (2,)
     product(G0, 4, 3, 5)
@@ -297,29 +314,28 @@
     for o1 in (0, 3, 1, 2):
         ag_ring2_end(0, o1)
     ag_ring2_end(1, 2)
-    product(G2, 4)
+    product(G2, 4, 3, 5)
     product(G0, 2, 6)
-    z_step(G2, 4)
+    z_far()
     z_step(G0, 2)
     product(G1, 2, 6)
     z_step(G1, 3)
-    product(G2, 3, 5)
-    z_step(G2, 3)
+    product(G2, 2, 6)
     product(G0, 1, 7)
+    z_step(G2, 2)
     z_step(G0, 1)
     product(G1, 1, 7)
     z_step(G1, 2)
-    product(G2, 2, 6)
-    z_step(G2, 2)
+    product(G2, 1, 7)
     product(G1, 0)
+    z_step(G2, 1)
     z_step(G1, 1)
-    product(G2, 1, 7)
-    z_step(G2, 1)
     product(G0, 0)
     product(G2, 0)
-    place(14, 16)
-    z_last(G0 + G1)
-    place(10, 14)
+    place(13, 16)
+    z_last(G0)
+    place(10, 13)
+    z_last(G1)
     z_last(G2)
 
     def cot_wait(i, _):
@@ -327,8 +343,7 @@
         return 0
 
     lax.fori_loop(1, 16, cot_wait, 0)
-    hidden = jnp.dot(wt[...], axb[...], preferred_element_type=F32)
-    hidden = hidden + jnp.dot(wt[...], axl[...], preferred_element_type=F32)
+    hidden = hid[...]
     sig = jax.nn.sigmoid(hidden)
     actb[...] = (hidden * sig).astype(BF)
     slope = cotb[...].astype(F32) * sig * (1.0 + hidden * (1.0 - sig))
@@ -336,36 +351,57 @@
     sll[...] = (slope - slb[...].astype(F32)).astype(BF)
     ORDER = (2, 1, 3, 0)
 
-    def gz_piece(side, dist, j):
-        owner = (z - dist + 8) % 8 if side == 0 else (z + dist) % 8
-        feats = pl.ds(pl.multiple_of((x + ORDER[j]) % 4 * 128, 128), 128)
-        return tg.at[owner, k, feats]
-
-    def gz_send(side, dist, j):
-        piece = gz_piece(side, dist, j)
-        send(piece, piece, gz_ss.at[side, dist, j], gz_rs.at[side, dist, j], at_z(1 if side == 0 else -1))
-
-    def gz_got(side, dist, j):
-        piece = gz_piece(side, dist, j)
-        got(piece, gz_ss.at[side, dist - 1, j], gz_rs.at[side, dist - 1, j], at_z(-1 if side == 0 else 1))
-
-    def gc_send(d):
-        piece = tg.at[(z + d) % 8, k]
-        send(piece, piece, gc_ss.at[d], gc_rs.at[d], twin)
-
-    def gc_got(d):
-        piece = tg.at[(z + d) % 8, 1 - k]
-        got(piece, gc_ss.at[d], gc_rs.at[d], twin)
-
-    for j in range(NS):
-        feats = pl.ds(pl.multiple_of((x + ORDER[j]) % 4 * 128, 128), 128)
+    def feats_of(o):
+        return pl.ds(pl.multiple_of((x + o) % 4 * 128, 128), 128)
+
+    def gz_piece(d, o, half=None):
+        start, size = (x + o) % 4 * 128, 128
+        if half is not None:
+            start, size = start + 64 * half, 64
+        return tg.at[(z + d + 8) % 8, k, pl.ds(pl.multiple_of(start, size), size)]
+
+    def gz_send(side, dist, o):
+        piece = gz_piece(-dist if side == 0 else dist, o, side if dist == 3 else None)
+        send(piece, piece, gz_ss.at[side, dist, o], gz_rs.at[side, dist, o], at_z(1 if side == 0 else -1))
+
+    def gz_got(side, dist, o):
+        piece = gz_piece(-dist if side == 0 else dist, o, side if dist == 4 else None)
+        got(piece, gz_ss.at[side, dist - 1, o], gz_rs.at[side, dist - 1, o], at_z(-1 if side == 0 else 1))
+
+    def gc_send(d, o):
+        piece = gz_piece(d, o)
+        send(piece, piece, gc_ss.at[o, d], gc_rs.at[o, d], twin)
+
+    def gc_got(d, o):
+        piece = tg.at[(z + d) % 8, 1 - k, feats_of(o)]
+        got(piece, gc_ss.at[o, d], gc_rs.at[o, d], twin)
+
+    def gather(o, dist):
+        for side in (0, 1):
+            gz_got(side, dist, o)
+            if dist < 4 and (o, dist) != (2, 2):
+                gz_send(side, dist, o)
+        for d in (4,) if dist == 4 else (dist, 8 - dist):
+            gc_send(d, o)
+
+    def gather_far():
+        for i, d in enumerate(FAR):
+            got(gz_piece(-d, 2), gf_ss.at[i], gf_rs.at[i], at_z(-d))
+            gc_send(8 - d, 2)
+
+    for o in ORDER:
+        feats = feats_of(o)
         tg[z, k, feats] = (
             jnp.dot(w_ref[feats], slb[...], preferred_element_type=F32)
             + jnp.dot(w_ref[feats], sll[...], preferred_element_type=F32)
         ).astype(BF)
         for side in (0, 1):
-            gz_send(side, 0, j)
-    gc_send(0)
+            gz_send(side, 0, o)
+        if o == 2:
+            for i, d in enumerate(FAR):
+                piece = gz_piece(0, 2)
+                send(piece, piece, gf_ss.at[i], gf_rs.at[i], at_z(d))
+        gc_send(0, o)
 
     def act_copy(i, peer, mine):
         return rc(
@@ -445,54 +481,20 @@
         send(wg_ref.at[:, k], wg_ref.at[:, k], w0_ss.at[1], w0_rs.at[1], twin)
         got(wg_ref.at[:, 1 - k], w0_ss.at[1], w0_rs.at[1], twin)
 
-    def z_rows(side, dist, j):
-        return dist < 4 or (j < NS // 2) == (side == 0)
-
-    def gather_step(dist):
-        for j in range(NS):
-            for side in (0, 1):
-                if not z_rows(side, dist, j):
-                    continue
-                gz_got(side, dist, j)
-                if dist < 4 and z_rows(side, dist + 1, j):
-                    gz_send(side, dist, j)
-        for d in (4,) if dist == 4 else (dist, 8 - dist):
-            gc_send(d)
-
-    def back_part(d):
-        block = (z + d) % 8
-        left = jnp.concatenate([tg[block, 0], tg[block, 1]], axis=1)
-        rows = pl.ds(pl.multiple_of(block * 256, 256), 256)
-        return jnp.dot(left, a[rows, :], preferred_element_type=F32)
-
-    gc_got(0)
-    acc[...] = back_part(0)
-    gather_step(1)
-    w_start_row()
-    place(6, 10)
-    gather_step(2)
-    for d in (1, 7):
-        gc_got(d)
-        acc[...] += back_part(d)
-    place(2, 6)
-    gather_step(3)
-    w_start_z()
-    for d in (2, 6):
-        gc_got(d)
-        acc[...] += back_part(d)
-    place(0, 2)
-    for d in (3, 5):
-        gc_got(d)
-        acc[...] += back_part(d)
-    gather_step(4)
-    gc_got(4)
-
-    def last_part(o):
-        block = (z + 4) % 8
-        feats = pl.ds(pl.multiple_of((x + o) % 4 * 128, 128), 128)
-        left = jnp.concatenate([tg[block, 0, feats], tg[block, 1, feats]], axis=1)
-        rows = pl.ds(pl.multiple_of(block * 256, 256), 256)
-        acc[feats] += jnp.dot(left, a[rows, :], preferred_element_type=F32)
+    def add_back(o, *ds):
+        feats = feats_of(o)
+        total = None
+        for d in ds:
+            gc_got(d, o)
+            block = (z + d) % 8
+            left = jnp.concatenate([tg[block, 0, feats], tg[block, 1, feats]], axis=1)
+            rows = pl.ds(pl.multiple_of(block * 256, 256), 256)
+            part = jnp.dot(left, a[rows, :], preferred_element_type=F32)
+            total = part if total is None else total + part
+        if 0 in ds:
+            acc[feats] = total
+        else:
+            acc[feats] += total
 
     def q_rows(h, o1, o2):
         if h == 0:
@@ -545,26 +547,56 @@
             value = value + xr2[h, o2 - 1].astype(F32)
         fg_ref[:, h * 1024 : (h + 1) * 1024] = value.astype(BF)
 
-    last_part(2)
+    gather(2, 1)
+    add_back(2, 0)
+    for o in (1, 3, 0):
+        gather(o, 1)
+    w_start_row()
+    place(6, 10)
+    gather(2, 2)
+    gather_far()
+    add_back(2, 1, 7)
+    for o in (1, 3, 0):
+        gather(o, 2)
+    place(0, 6)
+    add_back(2, 2, 6, 3, 5, 4)
     for o2 in ORDER:
         s1_halves(0, o2)
     s1_halves(1, 2)
     for o in (1, 3, 0):
-        last_part(o)
+        gather(o, 3)
+    w_start_z()
+    for o in (1, 3):
+        add_back(o, 0, 1, 7, 2, 6)
+    for j in (0, 1):
+        s1_pass(1, 2, j)
+    for o in (1, 3, 0):
+        gather(o, 4)
+    lax.fori_loop(1, 16, act_send, 0)
+    for o, j in ((1, 0), (3, 1)):
+        add_back(o, 3, 5, 4)
         s1_halves(1, o)
-    lax.fori_loop(1, 16, act_send, 0)
+        for o2 in ORDER:
+            s1_pass(0, o2, j)
+    s1_final(1, 2)
+    s2_send(1, 2)
+    add_back(0, 0, 1, 7, 2, 6, 3, 5, 4)
+    s1_halves(1, 0)
     act_ref[:, pl.ds(pl.multiple_of(c * 128, 128), 128)] = actb[pl.ds(pl.multiple_of(c * 32, 32), 32), :]
+    for o2 in (1, 3):
+        for j in (0, 1):
+            s1_pass(1, o2, j)
+    w_start_last()
     for o2 in ORDER:
-        for h in (0, 1):
-            for j in (0, 1):
-                s1_pass(h, o2, j)
-        if o2 == 1:
-            w_start_last()
-    for o2 in ORDER:
-        for h in (0, 1):
-            s1_final(h, o2)
-            if o2 > 0:
-                s2_send(h, o2)
+        s1_final(0, o2)
+        if o2 > 0:
+            s2_send(0, o2)
+    for j in (0, 1):
+        s1_pass(1, 0, j)
+    for o2 in (1, 3):
+        s1_final(1, o2)
+        s2_send(1, o2)
+    s1_final(1, 0)
     w_finish()
     wg_copy = pltpu.make_async_copy(wg_ref, wg_out, out_sem.at[0])
     wg_copy.start()
@@ -639,7 +671,9 @@
             vm((4, 8, 128, 128), F32),
             vm((2, 4, 4, 128, 128), BF),
             vm((2, 5, 4, 128, 128), BF),
-            vm((512, 128), BF),
+            vm((3, 128, 128), BF),
+            vm((3, 128, 128), BF),
+            vm((512, 128), F32),
             vm((512, 128), BF),
             vm((512, 128), BF),
             vm((512, 128), BF),
@@ -664,9 +698,11 @@
         + [dma((2, 5, 4))] * 2
         + [dma((4, 8))] * 2
         + [dma((2, 5, 4))] * 2
+        + [dma((3,))] * 2
         + [dma((16,))] * 2
-        + [dma((2, 4, NS))] * 2
-        + [dma((8,))] * 2
+        + [dma((2, 4, 4))] * 2
+        + [dma((3,))] * 2
+        + [dma((4, 8))] * 2
         + [dma((2, 5, 4))] * 2
         + [dma((2,))] * 2
         + [dma((16,))] * 2

time: 92.9 us -> 95.5 us (1.028)
  Pallas kernels: 92 us -> 94.6 us
    pallas_call x1, Pallas kernels: 89.2 us -> 91.8 us  [layer(): pl.pallas_call(layer_kernel, out_shape=(jax.ShapeDtypeStruct((32, 2048),...]
where the time goes in v6:
time: 95.5 us; the launch traced here: 95.4 us
  Pallas kernels  94.6 us (99%)
    pallas_call x1, Pallas kernels, layer(): pl.pallas_call(layer_kernel, out_shape=(jax.ShapeDtypeStruct((32, 2048),...  91.8 us
    pallas_call x1, Pallas kernels, finish(): pl.pallas_call(finish_kernel, out_shape=(jax.ShapeDtypeStruct((32, 2048),...  2.77 us

profile of v6, /device:TPU:1, one launch (start us, length us, event | category | flops | bytes accessed | tf_op | source)
XLA Modules:
  0.0 95.4 jit_solution(9478199465197731225)
XLA Ops:
  0.6 91.8 %layer.1 = (bf16[32,2048]{1,0:T(8,128)(2,1)}, bf16[32,2048]{1,0:T(8,128)(2,1)}, bf16[16,2,16,512]{3,2,1,0:T(8,128)(2,1)}) custom-call(s32[8,16]{1,0:T(8,128)} %bitcast.18, s32[1,16]{1,0:T(1,128)} %bitcast.19, s32[16,8,512]{2,1,0:T(8,128)} %bitcast.13, s32[16,8,512]{2,1,0:T(8,128)} %bitcast.14, bf16[16,8,512]{2,1,0:T(8,128)(2,1)} %bitcast.15, ...), custom_call_target="tpu_custom_call" | custom-call | tf_op jit(solution)/shard_map/layer/pallas_call | solution.py:640
  92.5 2.8 %finish.1 = (bf16[32,2048]{1,0:T(8,128)(2,1)}, bf16[32,2048]{1,0:T(8,128)(2,1)}, f32[512,512]{1,0:T(8,128)}) custom-call(bf16[32,2048]{1,0:T(8,128)(2,1)} %get-tuple-element.9.act_ref, bf16[32,2048]{1,0:T(8,128)(2,1)} %get-tuple-element.10.fg_ref, bf16[512,512]{1,0:T(8,128)(2,1)} %bitcast.12), custom_call_target="tpu_custom_call" | custom-call | tf_op jit(solution)/shard_map/finish/pallas_call | solution.py:738

commit v7 on v5

--- a/solution.py
+++ b/solution.py
@@ -17,7 +17,7 @@
     cols_in, counts_in, src_in, dst_in, ew_in, xt_in, cot_in, w_in,
     act_out, fg_out, wg_out,
     cols_ref, counts_ref, src_ref, dst_ref, ew_ref, xt_ref, cot_ref, w_ref, act_ref, fg_ref, wg_ref,
-    a, tiles, xg0, xg1, xg2, xg3, wt, cotb, pown, psend, precv, zr, zs, axb, axl, actb, slb, sll, tg, acc,
+    a, tiles, xg0, xg1, xg2, xg3, wt, cotb, pown, psend, precv, zr, zs, hid, axb, actb, slb, sll, tg, acc,
     xs1, xr1h, xr1f, s1, xs2, xr2,
     wp, w0r, w0s, w1r, wz,
     in_sem, out_sem,
@@ -67,12 +67,9 @@
 
     barrier = pltpu.get_barrier_semaphore()
 
-    def greet(i, _):
+    for i in (8, 7, 9, 6, 10, 5, 11, 4, 12, 3, 13, 2, 14, 1, 15):
+        pl.semaphore_signal(barrier, inc=1, device_id=(r, (c + i) % 16), device_id_type=MESH)
         pl.semaphore_signal(barrier, inc=1, device_id=((r + i) % 16, c), device_id_type=MESH)
-        pl.semaphore_signal(barrier, inc=1, device_id=(r, (c + i) % 16), device_id_type=MESH)
-        return 0
-
-    lax.fori_loop(1, 16, greet, 0)
     loads[0].wait()
     for b in range(16):
         xg0[b, y] = xt_ref[:, b * 128 : (b + 1) * 128]
@@ -125,14 +122,6 @@
     def place(start, stop):
         over(place_block, start, stop)
 
-    loads[1].wait()
-    eye = lax.broadcasted_iota(jnp.int32, (512, 512), 0) == lax.broadcasted_iota(jnp.int32, (512, 512), 1)
-    wt[...] = lax.dot_general(
-        jnp.where(eye, 1.0, 0.0).astype(BF), w_ref[...], NT, preferred_element_type=F32
-    ).astype(BF)
-    for load in loads[2:]:
-        load.wait()
-    make(0, 4)
     pl.semaphore_wait(barrier, 30)
 
     def xg_at(h, o1, o2):
@@ -200,10 +189,18 @@
         cot_copy(i, (c + i) % 16, c).start()
         return 0
 
+    loads[7].wait()
     lax.fori_loop(1, 16, cot_send, 0)
     cotb[pl.ds(pl.multiple_of(c * 32, 32), 32), :] = cot_ref[:, pl.ds(pl.multiple_of(c * 128, 128), 128)]
 
-    make(4, 7)
+    loads[1].wait()
+    eye = lax.broadcasted_iota(jnp.int32, (512, 512), 0) == lax.broadcasted_iota(jnp.int32, (512, 512), 1)
+    wt[...] = lax.dot_general(
+        jnp.where(eye, 1.0, 0.0).astype(BF), w_ref[...], NT, preferred_element_type=F32
+    ).astype(BF)
+    for load in loads[2:7]:
+        load.wait()
+    make(0, 4)
     for j, o in ((0, 3), (1, 1)):
         for h in (0, 1):
             ag_got(h, 0, 0, j)
@@ -213,7 +210,7 @@
     for h in (0, 1):
         ag_got(h, 0, 0, 2)
         ag_ring2_own(h, 2)
-    make(7, 10)
+    make(4, 8)
     for o1 in (3, 1):
         for h in (0, 1):
             ag_ring2_pass(h, o1)
@@ -276,17 +273,24 @@
             for side in (0, 1):
                 got(zr.at[side, 0, o], rz_ss.at[side, 1, o], rz_rs.at[side, 1, o], at_z(-1 if side == 0 else 1))
                 value = value + zr[side, 0, o].astype(F32)
-            rows = pl.ds(pl.multiple_of((x + o) % 4 * 128, 128), 128)
+            start = pl.multiple_of((x + o) % 4 * 128, 128)
             high = value.astype(BF)
-            axb[rows] = high
-            axl[rows] = (value - high.astype(F32)).astype(BF)
+            low = (value - high.astype(F32)).astype(BF)
+            axb[pl.ds(start, 128)] = high
+            weights = wt[:, pl.ds(start, 128)]
+            part = jnp.dot(
+                jnp.concatenate([weights, weights], axis=1),
+                jnp.concatenate([high, low], axis=0),
+                preferred_element_type=F32,
+            )
+            hid[...] = part if o == 0 else hid[...] + part
 
     G0, G1, G2 = (0,), (1, 3), (2,)
     product(G0, 4, 3, 5)
     z_step(G0, 4)
     for h in (0, 1):
         ag_ring2_pass(h, 2)
-    make(10, 13)
+    make(8, 13)
     for o1 in (3, 1):
         ag_ring2_end(1, o1)
     product(G1, 4)
@@ -294,13 +298,13 @@
     product(G1, 3, 5)
     z_step(G1, 4)
     make(13, 16)
+    product(G0, 2, 6)
     for o1 in (0, 3, 1, 2):
         ag_ring2_end(0, o1)
     ag_ring2_end(1, 2)
     product(G2, 4)
-    product(G0, 2, 6)
+    z_step(G0, 2)
     z_step(G2, 4)
-    z_step(G0, 2)
     product(G1, 2, 6)
     z_step(G1, 3)
     product(G2, 3, 5)
@@ -327,8 +331,7 @@
         return 0
 
     lax.fori_loop(1, 16, cot_wait, 0)
-    hidden = jnp.dot(wt[...], axb[...], preferred_element_type=F32)
-    hidden = hidden + jnp.dot(wt[...], axl[...], preferred_element_type=F32)
+    hidden = hid[...]
     sig = jax.nn.sigmoid(hidden)
     actb[...] = (hidden * sig).astype(BF)
     slope = cotb[...].astype(F32) * sig * (1.0 + hidden * (1.0 - sig))
@@ -639,7 +642,7 @@
             vm((4, 8, 128, 128), F32),
             vm((2, 4, 4, 128, 128), BF),
             vm((2, 5, 4, 128, 128), BF),
-            vm((512, 128), BF),
+            vm((512, 128), F32),
             vm((512, 128), BF),
             vm((512, 128), BF),
             vm((512, 128), BF),

time: 92.9 us -> 92.7 us (level)
  no operation moved by 1% of the time
where the time goes in v7:
time: 92.7 us; the launch traced here: 92.6 us
  Pallas kernels  91.8 us (99%)
    pallas_call x1, Pallas kernels, layer(): pl.pallas_call(layer_kernel, out_shape=(jax.ShapeDtypeStruct((32, 2048),...  89 us
    pallas_call x1, Pallas kernels, finish(): pl.pallas_call(finish_kernel, out_shape=(jax.ShapeDtypeStruct((32, 2048),...  2.77 us

profile of v7, /device:TPU:1, one launch (start us, length us, event | category | flops | bytes accessed | tf_op | source)
XLA Modules:
  0.0 92.6 jit_solution(16371798398088657433)
XLA Ops:
  0.6 89.0 %layer.1 = (bf16[32,2048]{1,0:T(8,128)(2,1)}, bf16[32,2048]{1,0:T(8,128)(2,1)}, bf16[16,2,16,512]{3,2,1,0:T(8,128)(2,1)}) custom-call(s32[8,16]{1,0:T(8,128)} %bitcast.18, s32[1,16]{1,0:T(1,128)} %bitcast.19, s32[16,8,512]{2,1,0:T(8,128)} %bitcast.13, s32[16,8,512]{2,1,0:T(8,128)} %bitcast.14, bf16[16,8,512]{2,1,0:T(8,128)(2,1)} %bitcast.15, ...), custom_call_target="tpu_custom_call" | custom-call | tf_op jit(solution)/shard_map/layer/pallas_call | solution.py:611
  89.6 2.8 %finish.1 = (bf16[32,2048]{1,0:T(8,128)(2,1)}, bf16[32,2048]{1,0:T(8,128)(2,1)}, f32[512,512]{1,0:T(8,128)}) custom-call(bf16[32,2048]{1,0:T(8,128)(2,1)} %get-tuple-element.9.act_ref, bf16[32,2048]{1,0:T(8,128)(2,1)} %get-tuple-element.10.fg_ref, bf16[512,512]{1,0:T(8,128)(2,1)} %bitcast.12), custom_call_target="tpu_custom_call" | custom-call | tf_op jit(solution)/shard_map/finish/pallas_call | solution.py:705

commit v8 on v7

--- a/solution.py
+++ b/solution.py
@@ -88,8 +88,8 @@
         for s in range(8):
             left = jnp.where(spots == spread(dst[s : s + 1]), spread(wts[s : s + 1]), BF(0))
             right = jnp.where(spots == spread(src[s : s + 1]), BF(1), BF(0))
-            tile = lax.dot_general(left, right, NT, preferred_element_type=F32)
-            tiles[g, :, s * 128 : (s + 1) * 128] = tile.astype(BF)
+            tile = lax.dot_general(right, left, NT, preferred_element_type=F32)
+            tiles[g, s * 128 : (s + 1) * 128] = tile.astype(BF)
 
     def place_block(g):
         names = [spread(jnp.full((1, 128), cols_ref[s, g].astype(F32), F32)) for s in range(8)]
@@ -97,11 +97,11 @@
         for j in range(16):
             here = BF(j)
             t = [
-                jnp.where(names[s] == here, tiles[g, :, s * 128 : (s + 1) * 128], BF(0))
+                jnp.where(names[s] == here, tiles[g, s * 128 : (s + 1) * 128], BF(0))
                 for s in range(8)
             ]
             total = ((t[0] + t[1]) + (t[2] + t[3])) + ((t[4] + t[5]) + (t[6] + t[7]))
-            a[rows, j * 128 : (j + 1) * 128] = total
+            a[j * 128 : (j + 1) * 128, rows] = total
 
     def nth_block(i):
         n = i // 2
@@ -223,7 +223,7 @@
             rows = [xg[o][col].reshape(128, 128) for o in offsets]
             picked.append(rows[0] if len(rows) == 1 else jnp.concatenate(rows, axis=0))
         left = jnp.concatenate(picked, axis=1)
-        return lax.dot_general(left, tiles[g], NT, preferred_element_type=F32)
+        return jnp.dot(left, tiles[g], preferred_element_type=F32)
 
     def product(offsets, *ds):
         for d in ds:
@@ -466,7 +466,7 @@
         block = (z + d) % 8
         left = jnp.concatenate([tg[block, 0], tg[block, 1]], axis=1)
         rows = pl.ds(pl.multiple_of(block * 256, 256), 256)
-        return jnp.dot(left, a[rows, :], preferred_element_type=F32)
+        return lax.dot_general(left, a[:, rows], NT, preferred_element_type=F32)
 
     gc_got(0)
     acc[...] = back_part(0)
@@ -490,12 +490,8 @@
     gather_step(4)
     gc_got(4)
 
-    def last_part(o):
-        block = (z + 4) % 8
-        feats = pl.ds(pl.multiple_of((x + o) % 4 * 128, 128), 128)
-        left = jnp.concatenate([tg[block, 0, feats], tg[block, 1, feats]], axis=1)
-        rows = pl.ds(pl.multiple_of(block * 256, 256), 256)
-        acc[feats] += jnp.dot(left, a[rows, :], preferred_element_type=F32)
+    acc[...] += back_part(4)
+    early = len(sent)
 
     def q_rows(h, o1, o2):
         if h == 0:
@@ -548,13 +544,9 @@
             value = value + xr2[h, o2 - 1].astype(F32)
         fg_ref[:, h * 1024 : (h + 1) * 1024] = value.astype(BF)
 
-    last_part(2)
     for o2 in ORDER:
         s1_halves(0, o2)
-    s1_halves(1, 2)
-    for o in (1, 3, 0):
-        last_part(o)
-        s1_halves(1, o)
+        s1_halves(1, o2)
     lax.fori_loop(1, 16, act_send, 0)
     act_ref[:, pl.ds(pl.multiple_of(c * 128, 128), 128)] = actb[pl.ds(pl.multiple_of(c * 32, 32), 32), :]
     for o2 in ORDER:
@@ -563,6 +555,8 @@
                 s1_pass(h, o2, j)
         if o2 == 1:
             w_start_last()
+    for copy in sent[:early]:
+        copy.wait_send()
     for o2 in ORDER:
         for h in (0, 1):
             s1_final(h, o2)
@@ -598,7 +592,7 @@
         return 0
 
     lax.fori_loop(1, 8, last_z, 0)
-    for copy in sent:
+    for copy in sent[early:]:
         copy.wait_send()
     for store in (wg_copy, act_store, fg_store):
         store.wait()
@@ -630,7 +624,7 @@
             vm((32, 2048), BF),
             vm((16, 2, 16, 512), BF),
             vm((2048, 2048), BF),
-            vm((16, 128, 1024), BF),
+            vm((16, 1024, 128), BF),
             vm((16, 4, 32, 128), BF),
             vm((16, 4, 32, 128), BF),
             vm((16, 4, 32, 128), BF),

time: 92.7 us -> 90.5 us (0.976)
  Pallas kernels: 91.8 us -> 89.5 us
    pallas_call x1, Pallas kernels: 89 us -> 86.8 us  [layer(): pl.pallas_call(layer_kernel, out_shape=(jax.ShapeDtypeStruct((32, 2048),...]
where the time goes in v8:
time: 90.5 us; the launch traced here: 90.3 us
  Pallas kernels  89.5 us (99%)
    pallas_call x1, Pallas kernels, layer(): pl.pallas_call(layer_kernel, out_shape=(jax.ShapeDtypeStruct((32, 2048),...  86.8 us
    pallas_call x1, Pallas kernels, finish(): pl.pallas_call(finish_kernel, out_shape=(jax.ShapeDtypeStruct((32, 2048),...  2.77 us

profile of v8, /device:TPU:1, one launch (start us, length us, event | category | flops | bytes accessed | tf_op | source)
XLA Modules:
  0.0 90.3 jit_solution(15716246709763877581)
XLA Ops:
  0.6 86.8 %layer.1 = (bf16[32,2048]{1,0:T(8,128)(2,1)}, bf16[32,2048]{1,0:T(8,128)(2,1)}, bf16[16,2,16,512]{3,2,1,0:T(8,128)(2,1)}) custom-call(s32[8,16]{1,0:T(8,128)} %bitcast.18, s32[1,16]{1,0:T(1,128)} %bitcast.19, s32[16,8,512]{2,1,0:T(8,128)} %bitcast.13, s32[16,8,512]{2,1,0:T(8,128)} %bitcast.14, bf16[16,8,512]{2,1,0:T(8,128)(2,1)} %bitcast.15, ...), custom_call_target="tpu_custom_call" | custom-call | tf_op jit(solution)/shard_map/layer/pallas_call | solution.py:605
  87.4 2.8 %finish.1 = (bf16[32,2048]{1,0:T(8,128)(2,1)}, bf16[32,2048]{1,0:T(8,128)(2,1)}, f32[512,512]{1,0:T(8,128)}) custom-call(bf16[32,2048]{1,0:T(8,128)(2,1)} %get-tuple-element.9.act_ref, bf16[32,2048]{1,0:T(8,128)(2,1)} %get-tuple-element.10.fg_ref, bf16[512,512]{1,0:T(8,128)(2,1)} %bitcast.12), custom_call_target="tpu_custom_call" | custom-call | tf_op jit(solution)/shard_map/finish/pallas_call | solution.py:699

commit v9 on v8

--- a/solution.py
+++ b/solution.py
@@ -22,7 +22,7 @@
     wp, w0r, w0s, w1r, wz,
     in_sem, out_sem,
     cot_ss, cot_rs, ag_ss, ag_rs, core_ss, core_rs, rz_ss, rz_rs,
-    act_ss, act_rs, gz_ss, gz_rs, gc_ss, gc_rs, rx_ss, rx_rs,
+    act_ss, act_rs, gz_ss, gz_rs, gc_ss, gc_rs, gd_ss, gd_rs, rx_ss, rx_rs,
     w0_ss, w0_rs, w1_ss, w1_rs, w2_ss, w2_rs, w3_ss, w3_rs,
 ):
     r = lax.axis_index("row")
@@ -451,6 +451,10 @@
     def z_rows(side, dist, j):
         return dist < 4 or (j < NS // 2) == (side == 0)
 
+    def far_piece(core, j):
+        feats = pl.ds(pl.multiple_of((x + ORDER[j]) % 4 * 128, 128), 128)
+        return tg.at[(z + 4) % 8, core, feats]
+
     def gather_step(dist):
         for j in range(NS):
             for side in (0, 1):
@@ -459,8 +463,11 @@
                 gz_got(side, dist, j)
                 if dist < 4 and z_rows(side, dist + 1, j):
                     gz_send(side, dist, j)
-        for d in (4,) if dist == 4 else (dist, 8 - dist):
-            gc_send(d)
+                if dist == 4:
+                    send(far_piece(k, j), far_piece(k, j), gd_ss.at[j], gd_rs.at[j], twin)
+        if dist < 4:
+            for d in (dist, 8 - dist):
+                gc_send(d)
 
     def back_part(d):
         block = (z + d) % 8
@@ -488,9 +495,9 @@
         gc_got(d)
         acc[...] += back_part(d)
     gather_step(4)
-    gc_got(4)
-
-    acc[...] += back_part(4)
+    for j in range(NS):
+        got(far_piece(1 - k, j), gd_ss.at[j], gd_rs.at[j], twin)
+
     early = len(sent)
 
     def q_rows(h, o1, o2):
@@ -544,9 +551,14 @@
             value = value + xr2[h, o2 - 1].astype(F32)
         fg_ref[:, h * 1024 : (h + 1) * 1024] = value.astype(BF)
 
-    for o2 in ORDER:
-        s1_halves(0, o2)
-        s1_halves(1, o2)
+    far = (z + 4) % 8
+    left = jnp.concatenate([tg[far, 0], tg[far, 1]], axis=1)
+    far_rows = pl.ds(pl.multiple_of(far * 256, 256), 256)
+    for h in (0, 1):
+        nodes = slice(h * 1024, (h + 1) * 1024)
+        acc[:, nodes] += lax.dot_general(left, a[nodes, far_rows], NT, preferred_element_type=F32)
+        for o2 in ORDER:
+            s1_halves(h, o2)
     lax.fori_loop(1, 16, act_send, 0)
     act_ref[:, pl.ds(pl.multiple_of(c * 128, 128), 128)] = actb[pl.ds(pl.multiple_of(c * 32, 32), 32), :]
     for o2 in ORDER:
@@ -664,6 +676,7 @@
         + [dma((16,))] * 2
         + [dma((2, 4, NS))] * 2
         + [dma((8,))] * 2
+        + [dma((NS,))] * 2
         + [dma((2, 5, 4))] * 2
         + [dma((2,))] * 2
         + [dma((16,))] * 2
@@ -676,22 +689,21 @@
     )(cols, counts, src, dst, ew, xt, cot, weight)
 
 
-def finish_kernel(act_ref, fg_ref, wg_ref, act_out, fg_out, wg_out, act_in, fg_in, wg_in, sems):
-    pairs = ((wg_ref, wg_in), (act_ref, act_in), (fg_ref, fg_in))
-    copies = [pltpu.make_async_copy(src, dst, sems.at[i]) for i, (src, dst) in enumerate(pairs)]
-    copies += [
-        pltpu.make_async_copy(act_in, act_out, sems.at[3]),
-        pltpu.make_async_copy(fg_in, fg_out, sems.at[4]),
-    ]
-    for copy in copies[:3]:
-        copy.start()
-    for i in (1, 2):
-        copies[i].wait()
-        copies[i + 2].start()
-    copies[0].wait()
-    wg_out[...] = wg_in[...].astype(F32)
-    copies[3].wait()
-    copies[4].wait()
+def finish_kernel(act_ref, fg_ref, wg_ref, act_out, fg_out, wg_out, act_in, fg_in, wg_in, wg_wide, sems):
+    rows = [pl.ds(128 * i, 128) for i in range(4)]
+    pairs = [(wg_ref.at[p], wg_in.at[p], wg_wide.at[p], wg_out.at[p]) for p in rows]
+    pairs += [(act_ref, act_in, act_in, act_out), (fg_ref, fg_in, fg_in, fg_out)]
+    loads = [pltpu.make_async_copy(p[0], p[1], sems.at[0, i]) for i, p in enumerate(pairs)]
+    stores = [pltpu.make_async_copy(p[2], p[3], sems.at[1, i]) for i, p in enumerate(pairs)]
+    for load in loads:
+        load.start()
+    for i in range(6):
+        loads[i].wait()
+        if i < 4:
+            wg_wide[rows[i]] = wg_in[rows[i]].astype(F32)
+        stores[i].start()
+    for store in stores:
+        store.wait()
 
 
 def finish(act, fg, wg):
@@ -704,12 +716,13 @@
             jax.ShapeDtypeStruct((512, 512), F32),
         ),
         in_specs=[anywhere] * 3,
-        out_specs=(anywhere, anywhere, pl.BlockSpec(memory_space=pltpu.VMEM)),
+        out_specs=(anywhere,) * 3,
         scratch_shapes=[
             pltpu.VMEM((32, 2048), BF),
             pltpu.VMEM((32, 2048), BF),
             pltpu.VMEM((512, 512), BF),
-            pltpu.SemaphoreType.DMA((5,)),
+            pltpu.VMEM((512, 512), F32),
+            pltpu.SemaphoreType.DMA((2, 6)),
         ],
         compiler_params=pltpu.CompilerParams(vmem_limit_bytes=58 << 20),
         name="finish",

time: 90.5 us -> 89.6 us (0.990)
  no operation moved by 1% of the time
where the time goes in v9:
time: 89.6 us; the launch traced here: 89.5 us
  Pallas kernels  88.7 us (99%)
    pallas_call x1, Pallas kernels, layer(): pl.pallas_call(layer_kernel, out_shape=(jax.ShapeDtypeStruct((32, 2048),...  86.7 us
    pallas_call x1, Pallas kernels, finish(): pl.pallas_call(finish_kernel, out_shape=(jax.ShapeDtypeStruct((32, 2048),...  2.07 us

profile of v9, /device:TPU:1, one launch (start us, length us, event | category | flops | bytes accessed | tf_op | source)
XLA Modules:
  0.0 89.5 jit_solution(5253869717231728682)
XLA Ops:
  0.6 86.7 %layer.1 = (bf16[32,2048]{1,0:T(8,128)(2,1)}, bf16[32,2048]{1,0:T(8,128)(2,1)}, bf16[16,2,16,512]{3,2,1,0:T(8,128)(2,1)}) custom-call(s32[8,16]{1,0:T(8,128)} %bitcast.18, s32[1,16]{1,0:T(1,128)} %bitcast.19, s32[16,8,512]{2,1,0:T(8,128)} %bitcast.13, s32[16,8,512]{2,1,0:T(8,128)} %bitcast.14, bf16[16,8,512]{2,1,0:T(8,128)(2,1)} %bitcast.15, ...), custom_call_target="tpu_custom_call" | custom-call | tf_op jit(solution)/shard_map/layer/pallas_call | solution.py:617
  87.3 2.1 %finish.1 = (bf16[32,2048]{1,0:T(8,128)(2,1)}, bf16[32,2048]{1,0:T(8,128)(2,1)}, f32[512,512]{1,0:T(8,128)}) custom-call(bf16[32,2048]{1,0:T(8,128)(2,1)} %get-tuple-element.9.act_ref, bf16[32,2048]{1,0:T(8,128)(2,1)} %get-tuple-element.10.fg_ref, bf16[512,512]{1,0:T(8,128)(2,1)} %bitcast.12), custom_call_target="tpu_custom_call" | custom-call | tf_op jit(solution)/shard_map/finish/pallas_call | solution.py:711

commit v10 on v9

--- a/solution.py
+++ b/solution.py
@@ -174,9 +174,9 @@
         for j in (0, 1):
             ag_send(h, 0, 0, j, 0, 0)
     for h in (0, 1):
+        ag_send(h, 0, 0, 2, 0, 0)
+    for h in (0, 1):
         ag_ring2_own(h, 0)
-    for h in (0, 1):
-        ag_send(h, 0, 0, 2, 0, 0)
 
     def cot_copy(i, peer, mine):
         return rc(
@@ -205,11 +205,11 @@
         for h in (0, 1):
             ag_got(h, 0, 0, j)
             ag_ring2_own(h, o)
-    for h in (1, 0):
-        ag_ring2_pass(h, 0)
     for h in (0, 1):
         ag_got(h, 0, 0, 2)
         ag_ring2_own(h, 2)
+    for h in (1, 0):
+        ag_ring2_pass(h, 0)
     make(4, 8)
     for o1 in (3, 1):
         for h in (0, 1):

time: 89.6 us -> 91.3 us (1.019)
  Pallas kernels: 88.7 us -> 90.4 us
    pallas_call x1, Pallas kernels: 86.7 us -> 88.4 us  [layer(): pl.pallas_call(layer_kernel, out_shape=(jax.ShapeDtypeStruct((32, 2048),...]
where the time goes in v10:
time: 91.3 us; the launch traced here: 91.2 us
  Pallas kernels  90.4 us (99%)
    pallas_call x1, Pallas kernels, layer(): pl.pallas_call(layer_kernel, out_shape=(jax.ShapeDtypeStruct((32, 2048),...  88.4 us
    pallas_call x1, Pallas kernels, finish(): pl.pallas_call(finish_kernel, out_shape=(jax.ShapeDtypeStruct((32, 2048),...  2.07 us

profile of v10, /device:TPU:1, one launch (start us, length us, event | category | flops | bytes accessed | tf_op | source)
XLA Modules:
  0.0 91.2 jit_solution(9388817400957479253)
XLA Ops:
  0.6 88.4 %layer.1 = (bf16[32,2048]{1,0:T(8,128)(2,1)}, bf16[32,2048]{1,0:T(8,128)(2,1)}, bf16[16,2,16,512]{3,2,1,0:T(8,128)(2,1)}) custom-call(s32[8,16]{1,0:T(8,128)} %bitcast.18, s32[1,16]{1,0:T(1,128)} %bitcast.19, s32[16,8,512]{2,1,0:T(8,128)} %bitcast.13, s32[16,8,512]{2,1,0:T(8,128)} %bitcast.14, bf16[16,8,512]{2,1,0:T(8,128)(2,1)} %bitcast.15, ...), custom_call_target="tpu_custom_call" | custom-call | tf_op jit(solution)/shard_map/layer/pallas_call | solution.py:617
  89.0 2.1 %finish.1 = (bf16[32,2048]{1,0:T(8,128)(2,1)}, bf16[32,2048]{1,0:T(8,128)(2,1)}, f32[512,512]{1,0:T(8,128)}) custom-call(bf16[32,2048]{1,0:T(8,128)(2,1)} %get-tuple-element.9.act_ref, bf16[32,2048]{1,0:T(8,128)(2,1)} %get-tuple-element.10.fg_ref, bf16[512,512]{1,0:T(8,128)(2,1)} %bitcast.12), custom_call_target="tpu_custom_call" | custom-call | tf_op jit(solution)/shard_map/finish/pallas_call | solution.py:711
